TPU v7x, 128 devices: a whole 4x4x4 slice. The times are simulated.
128 devices in a mesh: grp: 4 (over y), dev: 32 (over x, z, core).
Axes of the slice: x: 4, y: 4, z: 4, core: 2. Of those that a mesh axis runs over, the one named last changes fastest.
Arguments:
- captions: bfloat16 [32, 64, 4096], P('dev', 'grp'), may hold values from -6 to 6
- kv_weight: bfloat16 [4096, 2048], P('grp'), may hold values from -0.09375 to 0.09375
- image_tokens: bfloat16 [512, 256, 2048], P(('grp', 'dev')), may hold values from -28 to 28
- q_weight: bfloat16 [2048, 1024], replicated, may hold values from -0.125 to 0.125
- context_grad: bfloat16 [512, 256, 1024], P(('grp', 'dev')), may hold values from -6 to 6
- sample_prompt: int32 [512], replicated, may hold values from 0 to 31
- caption_len: int32 [32], replicated, may hold values from 8 to 64
Outputs:
- context: bfloat16 [512, 256, 1024], P(('grp', 'dev'))
- image_grad: bfloat16 [512, 256, 2048], P(('grp', 'dev'))
- caption_grad: float32 [32, 64, 4096], P('dev', 'grp')
Inputs may be any that keep to these rules, and one draw needn't show every extreme that they name: `sample_prompt`: sample s belongs to the device at position s // 4 of the devices taken with grp slowest; a prompt may have no samples.
All inputs are finite; a program needn't handle non-finite values.
Results may differ from a plain program's by a relative error of at most 0.008.
Values may be sent and summed in bfloat16 or wider, within the bound.
A program may use at most 128 MiB of HBM per device.

v0:
```python
import math

import jax
import jax.numpy as jnp
from jax import lax
from jax.sharding import PartitionSpec as P

HEADS = 8
HD = 128


NEG_FILL = -1e30


def attend_block(queries, key_rows, value_rows, live, grad_rows, score_scale):
    scores = (
        jnp.einsum("sihd,sjhd->shij", queries, key_rows, preferred_element_type=jnp.float32)
        * score_scale
    )
    scores = jnp.where(live[:, None, None, :], scores, NEG_FILL)
    top_score = jnp.max(scores, axis=-1, keepdims=True)
    expd = jnp.exp(scores - top_score)
    soft = expd / jnp.sum(expd, axis=-1, keepdims=True)
    soft_b = soft.astype(jnp.bfloat16)
    context = jnp.einsum(
        "shij,sjhd->sihd", soft_b, value_rows, preferred_element_type=jnp.float32
    ).astype(jnp.bfloat16)
    d_soft = jnp.einsum(
        "sihd,sjhd->shij", grad_rows, value_rows, preferred_element_type=jnp.float32
    )
    d_values = jnp.einsum("shij,sihd->sjhd", soft_b, grad_rows, preferred_element_type=jnp.float32)
    d_scores = (
        soft * (d_soft - jnp.sum(d_soft * soft, axis=-1, keepdims=True)) * score_scale
    ).astype(jnp.bfloat16)
    d_keys = jnp.einsum("shij,sihd->sjhd", d_scores, queries, preferred_element_type=jnp.float32)
    d_queries = jnp.einsum(
        "shij,sjhd->sihd", d_scores, key_rows, preferred_element_type=jnp.float32
    ).astype(jnp.bfloat16)
    return (context, d_queries, d_keys, d_values)


def shards(captions, kv_weight, image_tokens, q_weight, context_grad, sample_prompt, caption_len):
    n_grp = lax.axis_size("grp")
    n_dev = lax.axis_size("dev")
    grp_at = lax.axis_index("grp")
    dev_at = lax.axis_index("dev")
    samp_dev, img_len, width_img = image_tokens.shape
    prompt_dev, block_len, width_cap = captions.shape
    inner = q_weight.shape[1]
    full_len = block_len * n_grp
    prompts = prompt_dev * n_dev
    score_scale = 1.0 / math.sqrt(HD)
    whole_weight = lax.all_gather(kv_weight, "grp", axis=0, tiled=True)
    kv_block = jnp.dot(
        captions.reshape(prompt_dev * block_len, width_cap),
        whole_weight,
        preferred_element_type=jnp.float32,
    )
    kv_block = kv_block.astype(jnp.bfloat16).reshape(prompt_dev, block_len, 2 * inner)
    placed = sample_prompt.reshape(n_grp, n_dev, samp_dev)
    column = lax.dynamic_index_in_dim(placed, dev_at, 1, keepdims=False)
    own_prompts = lax.dynamic_index_in_dim(column, grp_at, 0, keepdims=False)
    whole_prompts = lax.all_gather(kv_block, "grp", axis=1, tiled=True)
    piece = lax.all_gather(whole_prompts, "dev", axis=0, tiled=True)
    prompt_rows = jnp.arange(piece.shape[0], dtype=jnp.int32)
    match = (own_prompts[:, None] == prompt_rows[None, :]).astype(jnp.bfloat16)
    picked = jnp.einsum("sp,plk->slk", match, piece, preferred_element_type=jnp.float32)
    sample_kv = picked.astype(jnp.bfloat16)
    prompt_ids = jnp.arange(prompts, dtype=jnp.int32)
    own_len = jnp.sum(
        jnp.where(own_prompts[:, None] == prompt_ids[None, :], caption_len[None, :], 0), axis=1
    )
    live = jnp.arange(full_len, dtype=jnp.int32)[None, :] < own_len[:, None]
    queries = jnp.dot(
        image_tokens.reshape(samp_dev * img_len, width_img),
        q_weight,
        preferred_element_type=jnp.float32,
    )
    queries = queries.astype(jnp.bfloat16).reshape(samp_dev, img_len, HEADS, HD)
    key_rows = sample_kv[:, :, :inner].reshape(samp_dev, full_len, HEADS, HD)
    value_rows = sample_kv[:, :, inner:].reshape(samp_dev, full_len, HEADS, HD)
    grad_rows = context_grad.reshape(samp_dev, img_len, HEADS, HD)
    context, d_queries, d_keys, d_values = attend_block(
        queries, key_rows, value_rows, live, grad_rows, score_scale
    )
    image_grad = jnp.dot(
        d_queries.reshape(samp_dev * img_len, inner), q_weight.T, preferred_element_type=jnp.float32
    )
    image_grad = image_grad.astype(jnp.bfloat16).reshape(samp_dev, img_len, width_img)
    grad_kv = jnp.concatenate(
        [d_keys.reshape(samp_dev, full_len, inner), d_values.reshape(samp_dev, full_len, inner)],
        axis=2,
    )
    split_grad = grad_kv.reshape(samp_dev, n_grp, block_len, 2 * inner)
    arrived = lax.all_to_all(split_grad, "grp", split_axis=1, concat_axis=1, tiled=True)
    prompt_rows = jnp.arange(lax.axis_size("dev") * prompt_dev, dtype=jnp.int32)
    match = (column[:, :, None] == prompt_rows[None, None, :]).astype(jnp.float32)
    kv_grad = lax.psum_scatter(
        jnp.einsum("gsp,sglk->plk", match, arrived, precision=lax.Precision.HIGHEST),
        "dev",
        scatter_dimension=0,
        tiled=True,
    )
    kv_grad_b = kv_grad.astype(jnp.bfloat16)
    caption_grad = jnp.dot(
        kv_grad_b.reshape(prompt_dev * block_len, 2 * inner),
        whole_weight.T,
        preferred_element_type=jnp.float32,
    )
    caption_grad = caption_grad.reshape(prompt_dev, block_len, width_cap)
    return (context.reshape(samp_dev, img_len, inner), image_grad, caption_grad)


def solution(mesh):
    placed = (
        P("dev", "grp", None),
        P("grp", None),
        P(("grp", "dev"), None, None),
        P(),
        P(("grp", "dev"), None, None),
        P(),
        P(),
    )
    return jax.shard_map(
        shards,
        mesh=mesh,
        in_specs=placed,
        out_specs=(
            P(("grp", "dev"), None, None),
            P(("grp", "dev"), None, None),
            P("dev", "grp", None),
        ),
        check_vma=False,
    )
```

profile of v0, /device:TPU:1, one launch (start us, length us, event | category | flops | bytes accessed | tf_op | source)
XLA Modules:
  0.0 407.2 jit_solution(1117545550551802118)
XLA Ops:
  7.2 0.7 all-gather.5.cloned.1.call-update
  8.0 159.0 %all-gather.5.cloned.1.call-done = bf16[4096,2048]{1,0:T(8,128)(2,1)} async-done(((bf16[1024,2048]{1,0:T(8,128)(2,1)}), bf16[4096,2048]{1,0:T(8,128)(2,1)}) %all-gather.5.cloned.1.call-update) | async-done | bytes 16777232 | tf_op jit(solution)/shard_map/all_gather | solution.py:53
  167.0 8.0 %convolution_convert_fusion.1 = bf16[16,2048]{1,0:T(8,128)(2,1)S(1)} fusion(bf16[4096,2048]{1,0:T(8,128)(2,1)} %all-gather.5.cloned.1.call-done, bf16[1,16,4096]{2,1,0:T(8,128)(2,1)S(1)} %copy-done.7), kind=kOutput, calls=%fused_computation.8 | convolution fusion | flops 268468224 | bytes 16973824 | tf_op jit(solution)/shard_map/dot_general | solution.py:54
  175.1 10.3 %all-gather = bf16[64,2048]{1,0:T(8,128)(2,1)} all-gather(bf16[16,2048]{1,0:T(8,128)(2,1)S(1)} %convolution_convert_fusion.1), channel_id=2, replica_groups=mesh['grp'=4,'dev'=32] {'grp'}, dimensions={0}, use_global_device_ids=true | all-gather | bytes 327680 | tf_op jit(solution)/shard_map/all_gather | solution.py:63
  185.5 8.0 %convert_bitcast_fusion.1 = bf16[128,8,8,128]{3,1,2,0:T(8,128)(2,1)S(1)} fusion(bf16[1024,2048]{1,0:T(8,128)(2,1)} %bitcast.98, bf16[2048,1024]{1,0:T(8,128)(2,1)} %param.10), kind=kOutput, calls=%fused_computation.24 | convolution fusion | flops 4296015872 | bytes 10485760 | tf_op jit(solution)/shard_map/dot_general | solution.py:74
  193.5 1.9 copy.53
  195.5 0.2 select_reduce_fusion
  195.7 46.1 %all-gather.7.cloned.1.call-done = bf16[2048,2048]{1,0:T(8,128)(2,1)} async-done(((bf16[64,2048]{1,0:T(8,128)(2,1)}), bf16[2048,2048]{1,0:T(8,128)(2,1)}) %all-gather.7.cloned.1.call-update) | async-done | bytes 8388624 | tf_op jit(solution)/shard_map/all_gather | solution.py:64
  241.9 12.7 %fusion.4 = bf16[4,64,2048]{2,0,1:T(4,128)(2,1)S(1)} fusion(bf16[32,64,2048]{2,1,0:T(8,128)(2,1)} %bitcast.92, s32[4]{0:T(128)S(1)} %dynamic-slice_bitcast_fusion), kind=kOutput, calls=%fused_computation.7 | convolution fusion | flops 34078848 | bytes 9437200 | tf_op jit(solution)/shard_map/sp,plk->slk/dot_general | solution.py:67
  254.6 0.4 fusion.54
  254.9 1.0 reshape.85
  255.9 0.2 reshape.82
  256.2 2.2 fusion.11
  258.3 4.0 fusion.55
  262.4 2.1 fusion.26
  264.4 5.2 %fusion.23 = f32[4,64,8,128]{3,1,2,0:T(8,128)S(1)} fusion(bf16[4,256,8,128]{3,2,1,0:T(8,128)(2,1)} %bitcast.94, f32[4,8,64,256]{3,2,1,0:T(8,128)} %fusion.11, f32[4,8,256,64]{2,3,1,0:T(8,128)} %get-tuple-element.15, f32[4,8,256]{2,1,0:T(8,128)S(1)} %get-tuple-element.14), kind=kOutput, calls=%fused_computation.33 | convolution fusion | flops 137896000 | bytes 7372800 | tf_op jit(solution)/shard_map/shij,sihd->sjhd/dot_general | solution.py:35
  269.7 0.6 copy.44
  270.3 0.2 concatenate.8
  270.5 0.6 copy.46
  271.4 2.7 copy.47
  274.1 4.0 all-to-all-start
  278.1 25.9 %all-to-all-done = f32[4,4,16,2048]{3,0,2,1:T(4,128)S(1)} async-done(((f32[4,4,16,2048]{3,0,2,1:T(4,128)}), f32[4,4,16,2048]{3,0,2,1:T(4,128)S(1)}, u32[]{:S(2)}, u32[]{:S(2)}) %all-to-all-start) | async-done | bytes 2097184 | tf_op jit(solution)/shard_map/all_to_all | solution.py:95
  304.0 2.3 convolution_bitcast_fusion.1
  306.3 4.4 %copy.49 = f32[32,16,2048]{2,1,0:T(8,128)} copy(f32[32,16,2048]{2,0,1:T(8,128)S(1)} %convolution_bitcast_fusion.1) | data formatting | bytes 8388608 | tf_op jit(solution)/shard_map/gsp,sglk->plk/dot_general | solution.py:99
  310.7 1.0 copy-done.6
  311.7 6.0 %convert_bitcast_fusion = bf16[4,256,8,128]{1,3,2,0:T(8,128)(2,1)} fusion(f32[4,8,64,256]{3,2,1,0:T(8,128)} %fusion.11, bf16[4,64,8,128]{3,2,0,1:T(8,128)(2,1)S(1)} %copy-done.6, f32[4,8,256,64]{2,3,1,0:T(8,128)} %get-tuple-element.15, f32[4,8,256]{2,1,0:T(8,128)S(1)} %get-tuple-element.14), kind=kOutput, calls=%fused_computation.21 | convolution fusion | flops 138944576 | bytes 6848512 | tf_op jit(solution)/shard_map/shij,sjhd->sihd/dot_general | solution.py:36
  317.7 4.4 %copy.42 = bf16[4,256,8,128]{3,2,1,0:T(8,128)(2,1)} copy(bf16[4,256,8,128]{1,3,2,0:T(8,128)(2,1)} %convert_bitcast_fusion) | data formatting | bytes 4194304 | tf_op jit(solution)/shard_map/convert_element_type | solution.py:38
  322.0 3.8 convolution_convert_fusion.2
  325.8 4.1 %copy.50 = bf16[4,256,1024]{2,1,0:T(8,128)(2,1)} copy(bf16[4,256,1024]{1,2,0:T(8,128)(2,1)} %bitcast.96) | data formatting | bytes 4194304
  330.0 8.4 %convolution_convert_fusion = bf16[1024,2048]{1,0:T(8,128)(2,1)} fusion(bf16[2048,1024]{1,0:T(8,128)(2,1)} %param.10, bf16[128,8,8,128]{3,2,1,0:T(8,128)(2,1)S(1)} %bitcast.95), kind=kOutput, calls=%fused_computation.5 | convolution fusion | flops 4297064448 | bytes 10485760 | tf_op jit(solution)/shard_map/dot_general | solution.py:86
  338.3 51.2 %reduce-scatter.2.cloned.1.call-done = f32[1,16,2048]{2,1,0:T(8,128)} async-done(((f32[32,16,2048]{2,1,0:T(8,128)}), f32[1,16,2048]{2,1,0:T(8,128)}) %reduce-scatter.2.cloned.1.call-update) | async-done | bytes 131088 | tf_op jit(solution)/shard_map/reduce_scatter | solution.py:98
  389.6 11.1 %convolution_bitcast_fusion = f32[1,16,4096]{2,1,0:T(8,128)} fusion(bf16[4096,2048]{1,0:T(8,128)(2,1)} %all-gather.5.cloned.1.call-done, f32[1,16,2048]{2,1,0:T(8,128)} %reduce-scatter.2.cloned.1.call-done), kind=kOutput, calls=%fused_computation.4 | convolution fusion | flops 268468224 | bytes 17170432 | tf_op jit(solution)/shard_map/dot_general | solution.py:105
  (30 shorter events, 0.7 us)
Async XLA Ops:
  7.2 249.0 %copy-start = (bf16[4,256,1024]{2,1,0:T(8,128)(2,1)S(1)}, bf16[4,256,1024]{2,1,0:T(8,128)(2,1)}, u32[]{:S(2)}) copy-start(bf16[4,256,1024]{2,1,0:T(8,128)(2,1)} %param.11) | copy-start | bytes 6291460
  7.2 159.8 %copy-start.7 = (bf16[1,16,4096]{2,1,0:T(8,128)(2,1)S(1)}, bf16[1,16,4096]{2,1,0:T(8,128)(2,1)}, u32[]{:S(2)}) copy-start(bf16[1,16,4096]{2,1,0:T(8,128)(2,1)} %param.7) | copy-start | bytes 393220
  7.2 159.8 %all-gather.5.cloned.1.call-start = ((), (), s32[]{:S(2)}) async-start(), calls=%async_computation.2 | async-start | bytes 20971520 | tf_op jit(solution)/shard_map/all_gather | solution.py:53
  7.9 177.5 %copy-start.8 = (s32[512]{0:T(512)S(1)}, s32[512]{0:T(512)}, u32[]{:S(2)}) copy-start(s32[512]{0:T(512)} %param.12) | copy-start | bytes 6148
  7.9 233.9 %all-gather.7.cloned.1.call-start = ((), (), s32[]{:S(2)}) async-start(), calls=%async_computation.4 | async-start | bytes 8650752 | tf_op jit(solution)/shard_map/all_gather | solution.py:64
  193.5 2.0 copy-start.9
  256.2 2.2 copy-start.2
  256.2 2.2 copy-start.5
  274.1 29.9 %all-to-all-start = ((f32[4,4,16,2048]{3,0,2,1:T(4,128)}), f32[4,4,16,2048]{3,0,2,1:T(4,128)S(1)}, u32[]{:S(2)}, u32[]{:S(2)}) async-start(f32[4,4,16,2048]{3,0,2,1:T(4,128)} %copy.47), calls=%async_computation | async-start | bytes 4194304 | tf_op jit(solution)/shard_map/all_to_all | solution.py:95
  278.1 111.5 %reduce-scatter.2.cloned.1.call-start = ((), (), s32[]{:S(2)}) async-start(), calls=%async_computation.3 | async-start | bytes 4325376 | tf_op jit(solution)/shard_map/reduce_scatter | solution.py:98
  310.6 1.0 copy-start.6
  317.7 4.4 %copy-start.3 = (bf16[4,64,8,128]{3,2,0,1:T(8,128)(2,1)S(1)}, bf16[4,64,8,128]{3,2,0,1:T(8,128)(2,1)}, u32[]{:S(2)}) copy-start(bf16[4,64,8,128]{3,2,0,1:T(8,128)(2,1)} %copy-done.2) | copy-start | bytes 1572868
  325.8 4.1 %copy-start.4 = (bf16[4,256,8,128]{3,2,1,0:T(8,128)(2,1)S(1)}, bf16[4,256,8,128]{3,2,1,0:T(8,128)(2,1)}, u32[]{:S(2)}) copy-start(bf16[4,256,8,128]{3,2,1,0:T(8,128)(2,1)} %copy.42) | copy-start | bytes 6291460
  389.6 11.1 %copy-start.1 = (bf16[4,256,1024]{2,1,0:T(8,128)(2,1)S(1)}, bf16[4,256,1024]{2,1,0:T(8,128)(2,1)}, u32[]{:S(2)}) copy-start(bf16[4,256,1024]{2,1,0:T(8,128)(2,1)} %param.11) | copy-start | bytes 6291460
Sparse Core Ops, SparseCore 0:
  9.7 157.2 all-gather.4
  185.5 56.2 all-gather.6
  310.8 78.7 reduce-scatter.1
where the time goes:
time: 409 us; the launch traced here: 407 us
  waiting for transfers between devices  283 us (69%)
  matrix products  73.8 us (18%)
  local copies, waits for them, and re-layouts  21.8 us (5%)
  between operations  13.9 us (3%)
  blocking collectives  10.3 us (3%)
    all_gather x1, waiting for transfers between devices, shards(): whole_weight = lax.all_gather(kv_weight, 'grp', axis=0, tiled=True)  159 us
    reduce_scatter x1, waiting for transfers between devices, shards(): lax.psum_scatter(jnp.einsum('gsp,sglk->plk', match, arrived, precision=la...  51.2 us
    all_gather x1, waiting for transfers between devices, shards(): piece = lax.all_gather(whole_prompts, 'dev', axis=0, tiled=True)  46.1 us
    all_to_all x1, waiting for transfers between devices, shards(): lax.all_to_all(split_grad, 'grp', split_axis=1, concat_axis=1, tiled=True)  25.9 us
    dot_general x1, matrix products, shards(): jnp.einsum('sp,plk->slk', match, piece, preferred_element_type=jnp.float32)  12.7 us
    dot_general x1, matrix products, shards(): jnp.dot(kv_grad_b.reshape(prompt_dev * block_len, 2 * inner), whole_weigh...  11.1 us
    all_gather x1, blocking collectives, shards(): whole_prompts = lax.all_gather(kv_block, 'grp', axis=1, tiled=True)  10.3 us
    dot_general x1, matrix products, shards(): jnp.dot(d_queries.reshape(samp_dev * img_len, inner), q_weight.T, preferr...  8.39 us
  transfers between devices with their start and end apart: 4, of which 4 were waited for; matrix products, arithmetic and copies ran while one was open for 9% of the time, Pallas kernels for 0%

commit v1 on v0

v1 whole, which is shorter than its diff:
```python
import functools
import math

import jax
import jax.numpy as jnp
from jax import lax
from jax.experimental import pallas as pl
from jax.experimental.pallas import tpu as pltpu
from jax.sharding import PartitionSpec as P

HEADS = 8
HD = 128
NEG_FILL = -1e30
MESH = pl.DeviceIdType.MESH
BF16 = jnp.bfloat16
F32 = jnp.float32
VMEM_LIMIT = 56 * 1024 * 1024

NY, NX, NZ, NC = 4, 4, 4, 2
SAMP = 4
TOK = 16
INNER = 1024
WIDE = 4096
DEPTH = 1024
IMG = 256
CIMG = 2048
PROMPTS = 32


def place():
    grp = lax.axis_index("grp")
    dev = lax.axis_index("dev")
    return grp, lax.div(dev, 8), lax.rem(lax.div(dev, 2), 4), lax.rem(dev, 2)


def at(grp, x, z, core):
    return {"grp": grp, "dev": (x * NZ + z) * NC + core}


def turn(index, step, size):
    return lax.rem(index + step, size)


def greet():
    y, x, z, c = place()
    barrier = pltpu.get_barrier_semaphore()
    peers = [at(turn(y, k, NY), x, z, turn(c, j, NC)) for k in range(NY) for j in range(NC) if k or j]
    peers += [at(y, turn(x, k, NX), z, c) for k in range(1, NX)]
    peers += [at(y, x, turn(z, k, NZ), c) for k in range(1, NZ)]
    for peer in peers:
        pl.semaphore_signal(barrier, inc=1, device_id=peer, device_id_type=MESH)
    pl.semaphore_wait(barrier, len(peers))


def send(src, dst, send_sem, recv_sem, peer):
    copy = pltpu.make_async_remote_copy(
        src_ref=src, dst_ref=dst, send_sem=send_sem, recv_sem=recv_sem, device_id=peer, device_id_type=MESH
    )
    copy.start()
    return copy


def front_kernel(
    prompt_ref, cap_ref, w_hbm, x_hbm, qw_hbm, q_out, kv_out,
    w_v, x_v, qw_v, q_v, caps, part, rs, kvb, gath, sel,
    load_sem, cap_s, cap_r, rs_s, rs_r, pair_s, pair_r, ag_s, ag_r, sel_s, sel_r, own_sem, q_sem,
):
    y, x, z, c = place()
    loads = [
        pltpu.make_async_copy(w_hbm, w_v, load_sem.at[0]),
        pltpu.make_async_copy(x_hbm, x_v, load_sem.at[1]),
        pltpu.make_async_copy(qw_hbm, qw_v, load_sem.at[2]),
    ]
    for load in loads:
        load.start()
    greet()

    def columns(index):
        return pl.ds(pl.multiple_of(index * DEPTH, DEPTH), DEPTH)

    sends = []
    for k in range(1, NY):
        to = turn(y, k, NY)
        sends.append(send(cap_ref.at[:, columns(to)], caps.at[y], cap_s.at[k], cap_r.at[k], at(to, x, z, c)))
    caps[pl.ds(y, 1)] = cap_ref[:, columns(y)][None]
    loads[0].wait()
    for copy in sends:
        copy.wait()

    lhs = caps[...].reshape(NY * TOK, DEPTH)
    sends = []
    step = 512
    for n in range(2 * INNER // step):
        cols = pl.ds(n * step, step)
        part[:, :, cols] = jnp.dot(lhs, w_v[:, cols], preferred_element_type=F32).reshape(NY, TOK, step)
        for k in range(1, NY):
            to = turn(y, k, NY)
            sends.append(
                send(part.at[to, :, cols], rs.at[k - 1, :, cols], rs_s.at[k, n], rs_r.at[k, n], at(to, x, z, c))
            )

    loads[1].wait()
    loads[2].wait()

    def project(tile):
        rows = pl.ds(tile * IMG, IMG)
        q_v[rows, :] = jnp.dot(x_v[rows, :], qw_v[...], preferred_element_type=F32).astype(BF16)
        copy = pltpu.make_async_copy(q_v.at[rows], q_out.at[rows], q_sem.at[tile])
        copy.start()
        return copy

    stores = [project(0)]
    for copy in sends:
        copy.wait()
    kvb[...] = (part[pl.ds(y, 1)][0] + rs[0] + rs[1] + rs[2]).astype(BF16)

    half = pl.ds(pl.multiple_of(c * INNER, INNER), INNER)
    other = pl.ds(pl.multiple_of((1 - c) * INNER, INNER), INNER)
    pair = send(kvb.at[:, other], gath.at[x, z, c], pair_s, pair_r, at(y, x, z, 1 - c))
    gath[x, z, c] = kvb[:, half]
    pair.wait()

    first, last = pl.ds(0, INNER // 2), pl.ds(INNER // 2, INNER // 2)
    sends = []
    for k in range(1, NX):
        own = gath.at[x, z, :, :, first]
        sends.append(send(own, own, ag_s.at[0, k], ag_r.at[0, k], at(y, turn(x, k, NX), z, c)))
        own = gath.at[x, z, :, :, last]
        sends.append(send(own, own, ag_s.at[1, k], ag_r.at[1, k], at(y, x, turn(z, k, NZ), c)))
    for copy in sends:
        copy.wait()
    sends = []
    for k in range(1, NX):
        own = gath.at[:, z, :, :, first]
        sends.append(send(own, own, ag_s.at[2, k], ag_r.at[2, k], at(y, x, turn(z, k, NZ), c)))
        own = gath.at[x, :, :, :, last]
        sends.append(send(own, own, ag_s.at[3, k], ag_r.at[3, k], at(y, turn(x, k, NX), z, c)))
    stores.append(project(1))
    stores.append(project(2))
    for copy in sends:
        copy.wait()

    sends = []
    for k in (1, 2, 3, 0):
        for j in range(NC):
            to_y, to_c = turn(y, k, NY), turn(c, j, NC)
            base = (to_y * (NX * NZ * NC) + (x * NZ + z) * NC + to_c) * SAMP
            for i in range(SAMP):
                p = prompt_ref[base + i]
                sel[k, j, i] = gath[lax.div(p, 8), lax.rem(lax.div(p, 2), 4), lax.rem(p, 2)]
            target = kv_out.at[:, y, :, half]
            if k or j:
                sends.append(send(sel.at[k, j], target, sel_s.at[k, j], sel_r.at[k, j], at(to_y, x, z, to_c)))
            else:
                own_copy = pltpu.make_async_copy(sel.at[k, j], target, own_sem)
                own_copy.start()
    stores.append(project(3))
    own_copy.wait()
    for copy in sends:
        copy.wait()
    for copy in stores:
        copy.wait()


def front(sample_prompt, captions, kv_weight, tokens, q_weight):
    any_space = pl.BlockSpec(memory_space=pl.ANY)
    vmem = pl.BlockSpec(memory_space=pltpu.VMEM)
    smem = pl.BlockSpec(memory_space=pltpu.SMEM)
    dma = pltpu.SemaphoreType.DMA
    return pl.pallas_call(
        front_kernel,
        out_shape=(
            jax.ShapeDtypeStruct((SAMP * IMG, INNER), BF16),
            jax.ShapeDtypeStruct((SAMP, NY, TOK, 2 * INNER), BF16),
        ),
        in_specs=[smem, vmem, any_space, any_space, any_space],
        out_specs=(any_space, any_space),
        scratch_shapes=[
            pltpu.VMEM((DEPTH, 2 * INNER), BF16),
            pltpu.VMEM((SAMP * IMG, CIMG), BF16),
            pltpu.VMEM((CIMG, INNER), BF16),
            pltpu.VMEM((SAMP * IMG, INNER), BF16),
            pltpu.VMEM((NY, TOK, DEPTH), BF16),
            pltpu.VMEM((NY, TOK, 2 * INNER), F32),
            pltpu.VMEM((NY - 1, TOK, 2 * INNER), F32),
            pltpu.VMEM((TOK, 2 * INNER), BF16),
            pltpu.VMEM((NX, NZ, NC, TOK, INNER), BF16),
            pltpu.VMEM((NY, NC, SAMP, TOK, INNER), BF16),
            dma((3,)),
            dma((NY,)), dma((NY,)),
            dma((NY, 4)), dma((NY, 4)),
            dma, dma,
            dma((4, NX)), dma((4, NX)),
            dma((NY, NC)), dma((NY, NC)),
            dma,
            dma((SAMP,)),
        ],
        compiler_params=pltpu.CompilerParams(
            collective_id=0, has_side_effects=True, vmem_limit_bytes=VMEM_LIMIT
        ),
    )(sample_prompt, captions, kv_weight, tokens, q_weight)


def attend_kernel(prompt_ref, len_ref, q_ref, grad_ref, kv_ref, qw_ref, context_ref, image_ref, dkv_ref, dq_v):
    grp = lax.axis_index("grp")
    dev = lax.axis_index("dev")
    sample = (grp * (NX * NZ * NC) + dev) * SAMP + pl.program_id(0)
    length = len_ref[prompt_ref[sample]]
    scale = 1.0 / math.sqrt(HD)
    live = lax.broadcasted_iota(jnp.int32, (NY * TOK, IMG), 0) < length
    for h in range(HEADS):
        cols = pl.ds(h * HD, HD)
        vcols = pl.ds(INNER + h * HD, HD)
        q = q_ref[:, cols]
        g = grad_ref[:, cols]
        key = kv_ref[:, cols]
        value = kv_ref[:, vcols]
        nt = (((1,), (1,)), ((), ()))
        tn = (((0,), (0,)), ((), ()))
        scores = lax.dot_general(key, q, nt, preferred_element_type=F32) * scale
        scores = jnp.where(live, scores, NEG_FILL)
        expd = jnp.exp(scores - jnp.max(scores, axis=0, keepdims=True))
        soft = expd * (1.0 / jnp.sum(expd, axis=0, keepdims=True))
        soft_b = soft.astype(BF16)
        d_soft = lax.dot_general(value, g, nt, preferred_element_type=F32)
        inner = jnp.sum(d_soft * soft, axis=0, keepdims=True)
        d_scores = (soft * (d_soft - inner) * scale).astype(BF16)
        context_ref[:, cols] = lax.dot_general(soft_b, value, tn, preferred_element_type=F32).astype(BF16)
        dq_v[:, cols] = lax.dot_general(d_scores, key, tn, preferred_element_type=F32).astype(BF16)
        dkv_ref[:, cols] = jnp.dot(d_scores, q, preferred_element_type=F32).astype(BF16)
        dkv_ref[:, vcols] = jnp.dot(soft_b, g, preferred_element_type=F32).astype(BF16)
    image_ref[...] = lax.dot_general(
        dq_v[...], qw_ref[...], (((1,), (1,)), ((), ())), preferred_element_type=F32
    ).astype(BF16)


def attend(sample_prompt, caption_len, queries, grads, kv, q_weight):
    smem = pl.BlockSpec(memory_space=pltpu.SMEM)
    full = NY * TOK
    return pl.pallas_call(
        attend_kernel,
        grid=(SAMP,),
        out_shape=(
            jax.ShapeDtypeStruct((SAMP, IMG, INNER), BF16),
            jax.ShapeDtypeStruct((SAMP, IMG, CIMG), BF16),
            jax.ShapeDtypeStruct((SAMP, full, 2 * INNER), BF16),
        ),
        in_specs=[
            smem,
            smem,
            pl.BlockSpec((None, IMG, INNER), lambda s: (s, 0, 0)),
            pl.BlockSpec((None, IMG, INNER), lambda s: (s, 0, 0)),
            pl.BlockSpec((None, full, 2 * INNER), lambda s: (s, 0, 0)),
            pl.BlockSpec((CIMG, INNER), lambda s: (0, 0)),
        ],
        out_specs=(
            pl.BlockSpec((None, IMG, INNER), lambda s: (s, 0, 0)),
            pl.BlockSpec((None, IMG, CIMG), lambda s: (s, 0, 0)),
            pl.BlockSpec((None, full, 2 * INNER), lambda s: (s, 0, 0)),
        ),
        scratch_shapes=[pltpu.VMEM((IMG, INNER), BF16)],
        compiler_params=pltpu.CompilerParams(vmem_limit_bytes=VMEM_LIMIT),
    )(sample_prompt, caption_len, queries, grads, kv, q_weight)


def back_kernel(
    prompt_ref, dkv_ref, w_hbm, out_ref,
    w_v, arr, sums, rsb, ra, rb, mid_a, mid_b, ta, tb, kvg, full, cg, cgr,
    load_sem, a_s, a_r, own_sem, r1_s, r1_r, r2_s, r2_r, f_s, f_r, o_s, o_r,
):
    y, x, z, c = place()
    load = pltpu.make_async_copy(w_hbm, w_v, load_sem)
    load.start()
    greet()

    def half_of(core):
        return pl.ds(pl.multiple_of(core * INNER, INNER), INNER)

    sends = []
    for k in (1, 2, 3, 0):
        for j in range(NC):
            to_y, to_c = turn(y, k, NY), turn(c, j, NC)
            piece = dkv_ref.at[:, to_y, :, half_of(to_c)]
            if k or j:
                sends.append(send(piece, arr.at[y, c], a_s.at[k, j], a_r.at[k, j], at(to_y, x, z, to_c)))
            else:
                own_copy = pltpu.make_async_copy(piece, arr.at[y, c], own_sem)
                own_copy.start()

    count = NY * NC * SAMP * TOK
    lanes = lax.broadcasted_iota(jnp.int32, (1, count), 1)
    owner = jnp.zeros((1, count), jnp.int32)
    for yy in range(NY):
        for cc in range(NC):
            for i in range(SAMP):
                spot = (yy * NC + cc) * SAMP + i
                p = prompt_ref[(yy * (NX * NZ * NC) + (x * NZ + z) * NC + cc) * SAMP + i]
                owner = jnp.where(lanes // TOK == spot, p, owner)
    wanted = owner * TOK + lanes % TOK
    rows = lax.broadcasted_iota(jnp.int32, (PROMPTS * TOK, count), 0)
    match = jnp.where(rows == wanted, 1.0, 0.0).astype(BF16)
    own_copy.wait()
    for copy in sends:
        copy.wait()
    total = jnp.dot(match, arr[...].reshape(count, INNER), preferred_element_type=F32)
    total = total.reshape(NX, NZ, NC, TOK, INNER)
    sums[...] = total
    rsb[...] = total.astype(BF16)

    first, last = pl.ds(0, INNER // 2), pl.ds(INNER // 2, INNER // 2)
    sends = []
    for k in range(1, NX):
        to = turn(x, k, NX)
        sends.append(send(rsb.at[to, :, :, :, first], ra.at[k - 1], r1_s.at[0, k], r1_r.at[0, k], at(y, to, z, c)))
        to = turn(z, k, NZ)
        sends.append(send(rsb.at[:, to, :, :, last], rb.at[k - 1], r1_s.at[1, k], r1_r.at[1, k], at(y, x, to, c)))
    for copy in sends:
        copy.wait()
    mid_a[...] = sums[x, :, :, :, first] + ra[0].astype(F32) + ra[1].astype(F32) + ra[2].astype(F32)
    for xx in range(NX):
        mid_b[xx] = sums[xx, z, :, :, last] + rb[0, xx].astype(F32) + rb[1, xx].astype(F32) + rb[2, xx].astype(F32)
    sends = []
    for k in range(1, NX):
        to = turn(z, k, NZ)
        sends.append(send(mid_a.at[to], ta.at[k - 1], r2_s.at[0, k], r2_r.at[0, k], at(y, x, to, c)))
        to = turn(x, k, NX)
        sends.append(send(mid_b.at[to], tb.at[k - 1], r2_s.at[1, k], r2_r.at[1, k], at(y, to, z, c)))
    for copy in sends:
        copy.wait()
    kvg[:, :, first] = (mid_a[z] + ta[0] + ta[1] + ta[2]).astype(BF16)
    kvg[:, :, last] = (mid_b[x] + tb[0] + tb[1] + tb[2]).astype(BF16)

    sends = []
    for k in range(NY):
        for j in range(NC):
            to_y, to_c = turn(y, k, NY), turn(c, j, NC)
            if k or j:
                sends.append(
                    send(kvg.at[to_c], full.at[y, :, half_of(c)], f_s.at[k, j], f_r.at[k, j], at(to_y, x, z, to_c))
                )
    full[y, :, half_of(c)] = kvg[c]
    load.wait()
    for copy in sends:
        copy.wait()
    cg[...] = lax.dot_general(
        full[...].reshape(NY * TOK, 2 * INNER), w_v[...], (((1,), (1,)), ((), ())), preferred_element_type=F32
    ).reshape(NY, TOK, DEPTH)
    sends = []
    for k in range(1, NY):
        to = turn(y, k, NY)
        sends.append(send(cg.at[to], cgr.at[y], o_s.at[k], o_r.at[k], at(to, x, z, c)))
    cgr[y] = cg[y]
    for copy in sends:
        copy.wait()
    for yy in range(NY):
        out_ref[:, pl.ds(yy * DEPTH, DEPTH)] = cgr[yy]


def back(sample_prompt, dkv, kv_weight):
    any_space = pl.BlockSpec(memory_space=pl.ANY)
    vmem = pl.BlockSpec(memory_space=pltpu.VMEM)
    smem = pl.BlockSpec(memory_space=pltpu.SMEM)
    dma = pltpu.SemaphoreType.DMA
    return pl.pallas_call(
        back_kernel,
        out_shape=jax.ShapeDtypeStruct((TOK, WIDE), F32),
        in_specs=[smem, any_space, any_space],
        out_specs=vmem,
        scratch_shapes=[
            pltpu.VMEM((DEPTH, 2 * INNER), BF16),
            pltpu.VMEM((NY, NC, SAMP, TOK, INNER), BF16),
            pltpu.VMEM((NX, NZ, NC, TOK, INNER), F32),
            pltpu.VMEM((NX, NZ, NC, TOK, INNER), BF16),
            pltpu.VMEM((NX - 1, NZ, NC, TOK, INNER // 2), BF16),
            pltpu.VMEM((NZ - 1, NX, NC, TOK, INNER // 2), BF16),
            pltpu.VMEM((NZ, NC, TOK, INNER // 2), F32),
            pltpu.VMEM((NX, NC, TOK, INNER // 2), F32),
            pltpu.VMEM((NZ - 1, NC, TOK, INNER // 2), F32),
            pltpu.VMEM((NX - 1, NC, TOK, INNER // 2), F32),
            pltpu.VMEM((NC, TOK, INNER), BF16),
            pltpu.VMEM((NY, TOK, 2 * INNER), BF16),
            pltpu.VMEM((NY, TOK, DEPTH), F32),
            pltpu.VMEM((NY, TOK, DEPTH), F32),
            dma,
            dma((NY, NC)), dma((NY, NC)),
            dma,
            dma((2, NX)), dma((2, NX)),
            dma((2, NX)), dma((2, NX)),
            dma((NY, NC)), dma((NY, NC)),
            dma((NY,)), dma((NY,)),
        ],
        compiler_params=pltpu.CompilerParams(
            collective_id=1, has_side_effects=True, vmem_limit_bytes=VMEM_LIMIT
        ),
    )(sample_prompt, dkv, kv_weight)


def shards(captions, kv_weight, image_tokens, q_weight, context_grad, sample_prompt, caption_len):
    queries, kv = front(
        sample_prompt,
        captions.reshape(TOK, WIDE),
        kv_weight,
        image_tokens.reshape(SAMP * IMG, CIMG),
        q_weight,
    )
    context, image_grad, dkv = attend(
        sample_prompt,
        caption_len,
        queries.reshape(SAMP, IMG, INNER),
        context_grad,
        kv.reshape(SAMP, NY * TOK, 2 * INNER),
        q_weight,
    )
    caption_grad = back(sample_prompt, dkv.reshape(SAMP, NY, TOK, 2 * INNER), kv_weight)
    return context, image_grad, caption_grad.reshape(1, TOK, WIDE)


def solution(mesh):
    placed = (
        P("dev", "grp", None),
        P("grp", None),
        P(("grp", "dev"), None, None),
        P(),
        P(("grp", "dev"), None, None),
        P(),
        P(),
    )
    return jax.shard_map(
        shards,
        mesh=mesh,
        in_specs=placed,
        out_specs=(
            P(("grp", "dev"), None, None),
            P(("grp", "dev"), None, None),
            P("dev", "grp", None),
        ),
        check_vma=False,
    )
```

time: 409 us -> 113 us (0.28)
  waiting for transfers between devices: 283 us -> 0 us
  Pallas kernels: 0 us -> 110 us
  matrix products: 73.8 us -> 0 us
  local copies, waits for them, and re-layouts: 21.8 us -> 1.67 us
  between operations: 13.9 us -> 0.65 us
  blocking collectives: 10.3 us -> 0 us
    all_gather x2 -> x0, waiting for transfers between devices: 205 us -> none  [the longest x1 159 us: shards(): whole_weight = lax.all_gather(kv_weight, 'grp', axis=0, tiled=True)]
    pallas_call x0 -> x3, Pallas kernels: none -> 110 us  [the longest x1 47.8 us: front(): pl.pallas_call(front_kernel, out_shape=(jax.ShapeDtypeStruct((SAMP * IMG,...]
    dot_general x11 -> x0, matrix products: 69.7 us -> none  [the longest x1 12.7 us: shards(): jnp.einsum('sp,plk->slk', match, piece, preferred_element_type=jnp.float32)]
    reduce_scatter x1 -> x0, waiting for transfers between devices: 51.2 us -> none  [shards(): lax.psum_scatter(jnp.einsum('gsp,sglk->plk', match, arrived, precision=la...]
    all_to_all x1 -> x0, waiting for transfers between devices: 25.9 us -> none  [shards(): lax.all_to_all(split_grad, 'grp', split_axis=1, concat_axis=1, tiled=True)]
    all_gather x1 -> x0, blocking collectives: 10.3 us -> none  [shards(): whole_prompts = lax.all_gather(kv_block, 'grp', axis=1, tiled=True)]
    unnamed x22 -> x1, local copies, waits for them, and re-layouts: 7.13 us -> 1.67 us
    convert_element_type x1 -> x0, local copies, waits for them, and re-layouts: 4.37 us -> none  [attend_block(): d_queries = jnp.einsum('shij,sjhd->sihd', d_scores, key_rows, preferred_e...]
  transfers between devices with their start and end apart: 4 -> 0, of which waited for: 4 -> 0; matrix products, arithmetic and copies ran while one was open for 9% -> 0% of each run, Pallas kernels for 0% -> 0%
where the time goes in v1:
time: 113 us
  Pallas kernels  110 us (97%)
  local copies, waits for them, and re-layouts  1.67 us (1%)
    pallas_call x1, Pallas kernels, front(): pl.pallas_call(front_kernel, out_shape=(jax.ShapeDtypeStruct((SAMP * IMG,...  47.8 us
    pallas_call x1, Pallas kernels, back(): pl.pallas_call(back_kernel, out_shape=jax.ShapeDtypeStruct((TOK, WIDE), F...  43.3 us
    pallas_call x1, Pallas kernels, attend(): pl.pallas_call(attend_kernel, grid=(SAMP,), out_shape=(jax.ShapeDtypeStru...  19.2 us

profile of v1, /device:TPU:1, one launch (start us, length us, event | category | flops | bytes accessed | tf_op | source)
XLA Modules:
  0.0 112.7 jit_solution(9811345465621726496)
XLA Ops:
  0.6 47.8 %shard_map.94 = (bf16[1024,1024]{1,0:T(8,128)(2,1)}, bf16[4,4,16,2048]{3,2,1,0:T(8,128)(2,1)}) custom-call(s32[512]{0:T(512)} %prompt_ref.5, bf16[16,4096]{1,0:T(8,128)(2,1)} %bitcast.11, bf16[1024,2048]{1,0:T(8,128)(2,1)} %w_hbm.3, bf16[1024,2048]{1,0:T(8,128)(2,1)} %bitcast.6, bf16[2048,1024]{1,0:T(8,128)(2,1)} %qw_ref.1), custom_call_target="tpu_custom_call" | custom-call | tf_op jit(solution)/shard_map/pallas_call | solution.py:170
  48.5 19.2 %shard_map.95 = (bf16[4,256,1024]{2,1,0:T(8,128)(2,1)}, bf16[4,256,2048]{2,1,0:T(8,128)(2,1)}, bf16[4,64,2048]{2,1,0:T(8,128)(2,1)}) custom-call(s32[512]{0:T(512)} %prompt_ref.5, s32[32]{0:T(128)} %len_ref.1, bf16[4,256,1024]{2,1,0:T(8,128)(2,1)} %bitcast.7, bf16[4,256,1024]{2,1,0:T(8,128)(2,1)} %grad_ref.1, bf16[4,64,2048]{2,1,0:T(8,128)(2,1)} %bitcast.10, ...), custom_call_target="tpu_custom_call" | custom-call | tf_op jit(solution)/shard_map/pallas_call | solution.py:240
  67.7 43.3 %shard_map.96 = f32[16,4096]{1,0:T(8,128)} custom-call(s32[512]{0:T(512)} %prompt_ref.5, bf16[4,4,16,2048]{3,2,1,0:T(8,128)(2,1)} %bitcast.8, bf16[1024,2048]{1,0:T(8,128)(2,1)} %w_hbm.3), custom_call_target="tpu_custom_call" | custom-call | tf_op jit(solution)/shard_map/pallas_call | solution.py:364
  111.0 1.7 %copy.11 = f32[1,16,4096]{2,1,0:T(8,128)} copy(f32[1,16,4096]{2,1,0:T(8,128)} %bitcast.9) | data formatting | bytes 524288

commit v2 on v0

v2 whole, which is shorter than its diff:
```python
import math

import jax
import jax.numpy as jnp
from jax import lax
from jax.experimental import pallas as pl
from jax.experimental.pallas import tpu as pltpu
from jax.sharding import PartitionSpec as P

HEADS = 8
HD = 128
NEG_FILL = -1e30
MESH = pl.DeviceIdType.MESH
BF16 = jnp.bfloat16
F32 = jnp.float32
VMEM_LIMIT = 56 * 1024 * 1024

NY, NX, NZ, NC = 4, 4, 4, 2
SAMP = 4
TOK = 16
INNER = 1024
WIDE = 4096
DEPTH = 1024
IMG = 256
CIMG = 2048
PROMPTS = 32
CHUNKS = 4
CW = INNER // CHUNKS
NT = (((1,), (1,)), ((), ()))
TN = (((0,), (0,)), ((), ()))


def place():
    grp = lax.axis_index("grp")
    dev = lax.axis_index("dev")
    return grp, lax.div(dev, 8), lax.rem(lax.div(dev, 2), 4), lax.rem(dev, 2)


def at(grp, x, z, core):
    return {"grp": grp, "dev": (x * NZ + z) * NC + core}


def turn(index, step, size):
    return lax.rem(index + step, size)


def greet():
    y, x, z, c = place()
    barrier = pltpu.get_barrier_semaphore()
    peers = [at(turn(y, k, NY), x, z, turn(c, j, NC)) for k in range(NY) for j in range(NC) if k or j]
    peers += [at(y, turn(x, k, NX), z, c) for k in range(1, NX)]
    peers += [at(y, x, turn(z, k, NZ), c) for k in range(1, NZ)]
    for peer in peers:
        pl.semaphore_signal(barrier, inc=1, device_id=peer, device_id_type=MESH)
    pl.semaphore_wait(barrier, len(peers))


def send(src, dst, send_sem, recv_sem, peer):
    copy = pltpu.make_async_remote_copy(
        src_ref=src, dst_ref=dst, send_sem=send_sem, recv_sem=recv_sem, device_id=peer, device_id_type=MESH
    )
    copy.start()
    return copy


def kernel(
    prompt_ref, len_ref, cap_hbm, w_hbm, x_hbm, qw_hbm, g_hbm, context_out, image_out, caption_out, *scratch
):
    (
        w_v, x_v, qw_v, q_v, g_v, ctx_v, dq_v, caps, part, rs, kvb, sel, skv, dkv, arr, match,
        sums, rsb, r1, mid, r2, kvg, full, cg,
        load_sem, cap_s, cap_r, rs_s, rs_r, pair_s, pair_r, ag_s, ag_r, sel_s, sel_r,
        grad_s, grad_r, r1_s, r1_r, r2_s, r2_r, f_s, f_r, o_s, o_r, store_sem,
    ) = scratch[:-CHUNKS]
    gath = scratch[-CHUNKS:]
    y, x, z, c = place()
    waits = []

    def push(src, dst, send_sem, recv_sem, peer):
        copy = send(src, dst, send_sem, recv_sem, peer)
        waits.append(copy.wait_send)
        return copy

    def columns(index):
        return pl.ds(pl.multiple_of(index * DEPTH, DEPTH), DEPTH)

    def keep(src, dst, sem):
        copy = pltpu.make_async_copy(src, dst, sem)
        copy.start()
        return copy

    own_cap = keep(cap_hbm.at[:, columns(y)], caps.at[y], load_sem.at[0])
    load_w = keep(w_hbm, w_v, load_sem.at[1])
    load_x = keep(x_hbm, x_v, load_sem.at[2])
    load_qw = keep(qw_hbm, qw_v, load_sem.at[3])
    load_g = keep(g_hbm, g_v, load_sem.at[4])
    greet()

    def project(tile):
        rows = pl.ds(tile * IMG, IMG)
        q_v[rows, :] = jnp.dot(x_v[rows, :], qw_v[...], preferred_element_type=F32).astype(BF16)

    arrive = []
    for k in range(1, NY):
        to = turn(y, k, NY)
        arrive.append(push(cap_hbm.at[:, columns(to)], caps.at[y], cap_s.at[k], cap_r.at[k], at(to, x, z, c)))
    load_x.wait()
    load_qw.wait()
    project(0)
    own_cap.wait()
    load_w.wait()
    for copy in arrive:
        copy.wait_recv()

    rs_copies = []
    for q in range(CHUNKS):
        lhs = caps[...].reshape(NY * TOK, DEPTH)
        for half in range(2):
            part[q, :, :, pl.ds(half * CW, CW)] = jnp.dot(
                lhs, w_v[:, pl.ds(half * INNER + q * CW, CW)], preferred_element_type=F32
            ).reshape(NY, TOK, CW)
        copies = []
        for k in range(1, NY):
            to = turn(y, k, NY)
            copies.append(push(part.at[q, to], rs.at[q, k - 1], rs_s.at[q, k], rs_r.at[q, k], at(to, x, z, c)))
        rs_copies.append(copies)
    project(1)

    pair_copies = []
    for q in range(CHUNKS):
        for copy in rs_copies[q]:
            copy.wait_recv()
        whole = (part[q, y] + rs[q, 0] + rs[q, 1] + rs[q, 2]).astype(BF16)
        kvb[q, 0] = whole[:, :CW]
        kvb[q, 1] = whole[:, CW:]
        pair_copies.append(
            push(kvb.at[q, 1 - c], gath[q].at[x, z, c], pair_s.at[q], pair_r.at[q], at(y, x, z, 1 - c))
        )
        gath[q][x, z, c] = kvb[q, c]

    def over(axis, k):
        return (turn(x, k, NX), at(y, turn(x, k, NX), z, c)) if axis == 0 else (
            turn(z, k, NZ), at(y, x, turn(z, k, NZ), c))

    first_copies = []
    for q in range(CHUNKS):
        pair_copies[q].wait_recv()
        own = gath[q].at[x, z]
        first_copies.append(
            [push(own, own, ag_s.at[0, q, k], ag_r.at[0, q, k], over(q % 2, k)[1]) for k in range(1, NX)]
        )
    project(2)
    second_copies = []
    for q in range(CHUNKS):
        for copy in first_copies[q]:
            copy.wait_recv()
        own = gath[q].at[:, z] if q % 2 == 0 else gath[q].at[x]
        second_copies.append(
            [push(own, own, ag_s.at[1, q, k], ag_r.at[1, q, k], over(1 - q % 2, k)[1]) for k in range(1, NX)]
        )
    project(3)

    sel_copies = []
    for q in range(CHUNKS):
        for copy in second_copies[q]:
            copy.wait_recv()
        copies = []
        for k in (2, 1, 3, 0):
            for j in range(NC):
                to_y, to_c = turn(y, k, NY), turn(c, j, NC)
                base = (to_y * (NX * NZ * NC) + (x * NZ + z) * NC + to_c) * SAMP
                for i in range(SAMP):
                    p = prompt_ref[base + i]
                    block = gath[q][lax.div(p, 8), lax.rem(lax.div(p, 2), 4), lax.rem(p, 2)]
                    if k or j:
                        sel[q, k, j, i] = block
                    else:
                        skv[q, c, i, y] = block
                if k or j:
                    copies.append(
                        push(
                            sel.at[q, k, j], skv.at[q, c, :, y], sel_s.at[q, k, j], sel_r.at[q, k, j],
                            at(to_y, x, z, to_c),
                        )
                    )
        sel_copies.append(copies)
    load_g.wait()

    count = NY * NC * SAMP * TOK
    lanes = lax.broadcasted_iota(jnp.int32, (1, count), 1)
    owner = jnp.zeros((1, count), jnp.int32)
    for yy in range(NY):
        for cc in range(NC):
            for i in range(SAMP):
                spot = (yy * NC + cc) * SAMP + i
                p = prompt_ref[(yy * (NX * NZ * NC) + (x * NZ + z) * NC + cc) * SAMP + i]
                owner = jnp.where(lanes // TOK == spot, p, owner)
    wanted = owner * TOK + lanes % TOK
    ids = lax.broadcasted_iota(jnp.int32, (PROMPTS * TOK, count), 0)
    match[...] = jnp.where(ids == wanted, 1.0, 0.0).astype(BF16)

    scale = 1.0 / math.sqrt(HD)
    base = (y * (NX * NZ * NC) + (x * NZ + z) * NC + c) * SAMP
    tokens = NY * TOK

    def attention(q, s):
        rows = pl.ds(pl.multiple_of(s * IMG, IMG), IMG)
        cols = pl.ds(q * CW, CW)
        length = len_ref[prompt_ref[base + s]]
        live = lax.broadcasted_iota(jnp.int32, (2, tokens, IMG), 1) < length
        lead = lax.broadcasted_iota(jnp.int32, (tokens, CW), 1) < HD
        queries = q_v[rows, cols]
        grads = g_v[rows, cols]
        key = skv[q, 0, s].reshape(tokens, CW)
        value = skv[q, 1, s].reshape(tokens, CW)
        zero = jnp.zeros_like(key)
        key2 = jnp.concatenate([jnp.where(lead, key, zero), jnp.where(lead, zero, key)], axis=0)
        value2 = jnp.concatenate([jnp.where(lead, value, zero), jnp.where(lead, zero, value)], axis=0)
        scores = lax.dot_general(key2, queries, NT, preferred_element_type=F32) * scale
        scores = jnp.where(live, scores.reshape(2, tokens, IMG), NEG_FILL)
        expd = jnp.exp(scores - jnp.max(scores, axis=1, keepdims=True))
        soft = expd * (1.0 / jnp.sum(expd, axis=1, keepdims=True))
        soft_b = soft.astype(BF16).reshape(2 * tokens, IMG)
        d_soft = lax.dot_general(value2, grads, NT, preferred_element_type=F32).reshape(2, tokens, IMG)
        inner = jnp.sum(d_soft * soft, axis=1, keepdims=True)
        d_scores = (soft * (d_soft - inner) * scale).astype(BF16).reshape(2 * tokens, IMG)
        ctx_v[rows, cols] = lax.dot_general(soft_b, value2, TN, preferred_element_type=F32).astype(BF16)
        dq_v[rows, cols] = lax.dot_general(d_scores, key2, TN, preferred_element_type=F32).astype(BF16)
        d_key = jnp.dot(d_scores, queries, preferred_element_type=F32)
        d_value = jnp.dot(soft_b, grads, preferred_element_type=F32)
        dkv[q, 0, s] = jnp.where(lead, d_key[:tokens], d_key[tokens:]).astype(BF16).reshape(NY, TOK, CW)
        dkv[q, 1, s] = jnp.where(lead, d_value[:tokens], d_value[tokens:]).astype(BF16).reshape(NY, TOK, CW)

    grad_copies, r1_copies, r2_copies, f_copies = {}, {}, {}, {}

    def attend(q):
        for copy in sel_copies[q]:
            copy.wait_recv()

        def two(t, carry):
            attention(q, 2 * t)
            attention(q, 2 * t + 1)
            return carry

        lax.fori_loop(0, SAMP // 2, two, 0)
        copies = []
        for k in (2, 1, 3, 0):
            for j in range(NC):
                to_y, to_c = turn(y, k, NY), turn(c, j, NC)
                if k or j:
                    copies.append(
                        push(
                            dkv.at[q, to_c, :, to_y], arr.at[q, y, c], grad_s.at[q, k, j], grad_r.at[q, k, j],
                            at(to_y, x, z, to_c),
                        )
                    )
        arr[q, y, c] = dkv[q, c, :, y]
        grad_copies[q] = copies
        cols = pl.ds(q * CW, CW)
        waits.append(keep(ctx_v.at[:, cols], context_out.at[:, cols], store_sem.at[q]).wait)

    def add_up(q):
        for copy in grad_copies[q]:
            copy.wait_recv()
        total = jnp.dot(match[...], arr[q].reshape(count, CW), preferred_element_type=F32)
        total = total.reshape(NX, NZ, NC, TOK, CW)
        sums[q] = total
        rsb[q] = total.astype(BF16)
        copies = []
        for k in range(1, NX):
            to, peer = over(q % 2, k)
            piece = rsb.at[q, to] if q % 2 == 0 else rsb.at[q, :, to]
            copies.append(push(piece, r1.at[q, k - 1], r1_s.at[q, k], r1_r.at[q, k], peer))
        r1_copies[q] = copies

    def scatter(q):
        for copy in r1_copies[q]:
            copy.wait_recv()
        own = sums[q, x] if q % 2 == 0 else sums[q, :, z]
        mid[q] = own + r1[q, 0].astype(F32) + r1[q, 1].astype(F32) + r1[q, 2].astype(F32)
        copies = []
        for k in range(1, NX):
            to, peer = over(1 - q % 2, k)
            copies.append(push(mid.at[q, to], r2.at[q, k - 1], r2_s.at[q, k], r2_r.at[q, k], peer))
        r2_copies[q] = copies

    def spread(q):
        for copy in r2_copies[q]:
            copy.wait_recv()
        own = mid[q, z] if q % 2 == 0 else mid[q, x]
        kvg[q] = (own + r2[q, 0] + r2[q, 1] + r2[q, 2]).astype(BF16)
        copies = []
        for k in (2, 1, 3, 0):
            for j in range(NC):
                to_y, to_c = turn(y, k, NY), turn(c, j, NC)
                if k or j:
                    copies.append(
                        push(
                            kvg.at[q, to_c], full.at[q, c, y], f_s.at[q, k, j], f_r.at[q, k, j],
                            at(to_y, x, z, to_c),
                        )
                    )
        full[q, c, y] = kvg[q, c]
        f_copies[q] = copies

    def finish(q):
        for copy in f_copies[q]:
            copy.wait_recv()
        term = None
        for half in range(2):
            more = lax.dot_general(
                full[q, half].reshape(tokens, CW), w_v[:, pl.ds(half * INNER + q * CW, CW)], NT,
                preferred_element_type=F32,
            )
            term = more if term is None else term + more
        term = term.reshape(NY, TOK, DEPTH)
        cg[...] = term if q == 0 else cg[...] + term

    def image(tile):
        rows = pl.ds(tile * IMG, IMG)
        x_v[rows, :] = lax.dot_general(dq_v[rows, :], qw_v[...], NT, preferred_element_type=F32).astype(BF16)
        waits.append(keep(x_v.at[rows], image_out.at[rows], store_sem.at[CHUNKS + tile]).wait)

    attend(0)
    attend(1)
    add_up(0)
    attend(2)
    add_up(1)
    scatter(0)
    attend(3)
    add_up(2)
    scatter(1)
    spread(0)
    image(0)
    add_up(3)
    scatter(2)
    spread(1)
    finish(0)
    image(1)
    scatter(3)
    spread(2)
    finish(1)
    image(2)
    spread(3)
    finish(2)
    image(3)
    finish(3)
    arrive = []
    for k in range(1, NY):
        to = turn(y, k, NY)
        arrive.append(push(cg.at[to], caption_out.at[:, columns(y)], o_s.at[k], o_r.at[k], at(to, x, z, c)))
    waits.append(keep(cg.at[y], caption_out.at[:, columns(y)], store_sem.at[CHUNKS + SAMP]).wait)
    for copy in arrive:
        copy.wait_recv()
    for wait in waits:
        wait()


def shards(captions, kv_weight, image_tokens, q_weight, context_grad, sample_prompt, caption_len):
    any_space = pl.BlockSpec(memory_space=pl.ANY)
    smem = pl.BlockSpec(memory_space=pltpu.SMEM)
    dma = pltpu.SemaphoreType.DMA
    rows = SAMP * IMG

    def pair(*shape):
        return [dma(shape), dma(shape)]

    context, image_grad, caption_grad = pl.pallas_call(
        kernel,
        out_shape=(
            jax.ShapeDtypeStruct((rows, INNER), BF16),
            jax.ShapeDtypeStruct((rows, CIMG), BF16),
            jax.ShapeDtypeStruct((TOK, WIDE), F32),
        ),
        in_specs=[smem, smem] + [any_space] * 5,
        out_specs=(any_space,) * 3,
        scratch_shapes=[
            pltpu.VMEM((DEPTH, 2 * INNER), BF16),
            pltpu.VMEM((rows, CIMG), BF16),
            pltpu.VMEM((CIMG, INNER), BF16),
            pltpu.VMEM((rows, INNER), BF16),
            pltpu.VMEM((rows, INNER), BF16),
            pltpu.VMEM((rows, INNER), BF16),
            pltpu.VMEM((rows, INNER), BF16),
            pltpu.VMEM((NY, TOK, DEPTH), BF16),
            pltpu.VMEM((CHUNKS, NY, TOK, 2 * CW), F32),
            pltpu.VMEM((CHUNKS, NY - 1, TOK, 2 * CW), F32),
            pltpu.VMEM((CHUNKS, 2, TOK, CW), BF16),
            pltpu.VMEM((CHUNKS, NY, NC, SAMP, TOK, CW), BF16),
            pltpu.VMEM((CHUNKS, 2, SAMP, NY, TOK, CW), BF16),
            pltpu.VMEM((CHUNKS, 2, SAMP, NY, TOK, CW), BF16),
            pltpu.VMEM((CHUNKS, NY, NC, SAMP, TOK, CW), BF16),
            pltpu.VMEM((PROMPTS * TOK, NY * NC * SAMP * TOK), BF16),
            pltpu.VMEM((CHUNKS, NX, NZ, NC, TOK, CW), F32),
            pltpu.VMEM((CHUNKS, NX, NZ, NC, TOK, CW), BF16),
            pltpu.VMEM((CHUNKS, NX - 1, NZ, NC, TOK, CW), BF16),
            pltpu.VMEM((CHUNKS, NZ, NC, TOK, CW), F32),
            pltpu.VMEM((CHUNKS, NZ - 1, NC, TOK, CW), F32),
            pltpu.VMEM((CHUNKS, NC, TOK, CW), BF16),
            pltpu.VMEM((CHUNKS, 2, NY, TOK, CW), BF16),
            pltpu.VMEM((NY, TOK, DEPTH), F32),
            dma((5,)),
            *pair(NY),
            *pair(CHUNKS, NY),
            *pair(CHUNKS),
            *pair(2, CHUNKS, NX),
            *pair(CHUNKS, NY, NC),
            *pair(CHUNKS, NY, NC),
            *pair(CHUNKS, NX),
            *pair(CHUNKS, NX),
            *pair(CHUNKS, NY, NC),
            *pair(NY),
            dma((CHUNKS + SAMP + 1,)),
        ] + [pltpu.VMEM((NX, NZ, NC, TOK, CW), BF16) for _ in range(CHUNKS)],
        compiler_params=pltpu.CompilerParams(
            collective_id=0, has_side_effects=True, vmem_limit_bytes=VMEM_LIMIT
        ),
    )(
        sample_prompt,
        caption_len,
        captions.reshape(TOK, WIDE),
        kv_weight,
        image_tokens.reshape(rows, CIMG),
        q_weight,
        context_grad.reshape(rows, INNER),
    )
    return (
        context.reshape(SAMP, IMG, INNER),
        image_grad.reshape(SAMP, IMG, CIMG),
        caption_grad.reshape(1, TOK, WIDE),
    )


def solution(mesh):
    placed = (
        P("dev", "grp", None),
        P("grp", None),
        P(("grp", "dev"), None, None),
        P(),
        P(("grp", "dev"), None, None),
        P(),
        P(),
    )
    return jax.shard_map(
        shards,
        mesh=mesh,
        in_specs=placed,
        out_specs=(
            P(("grp", "dev"), None, None),
            P(("grp", "dev"), None, None),
            P("dev", "grp", None),
        ),
        check_vma=False,
    )
```

time: 409 us -> 86.1 us (0.21)
  waiting for transfers between devices: 283 us -> 0 us
  Pallas kernels: 0 us -> 79.4 us
  matrix products: 73.8 us -> 0 us
  local copies, waits for them, and re-layouts: 21.8 us -> 5.96 us
  between operations: 13.9 us -> 0.65 us
  blocking collectives: 10.3 us -> 0 us
    all_gather x2 -> x0, waiting for transfers between devices: 205 us -> none  [the longest x1 159 us: shards(): whole_weight = lax.all_gather(kv_weight, 'grp', axis=0, tiled=True)]
    pallas_call x0 -> x1, Pallas kernels: none -> 79.4 us  [shards(): pl.pallas_call(kernel, out_shape=(jax.ShapeDtypeStruct((rows, INNER), BF1...]
    dot_general x11 -> x0, matrix products: 69.7 us -> none  [the longest x1 12.7 us: shards(): jnp.einsum('sp,plk->slk', match, piece, preferred_element_type=jnp.float32)]
    reduce_scatter x1 -> x0, waiting for transfers between devices: 51.2 us -> none  [shards(): lax.psum_scatter(jnp.einsum('gsp,sglk->plk', match, arrived, precision=la...]
    all_to_all x1 -> x0, waiting for transfers between devices: 25.9 us -> none  [shards(): lax.all_to_all(split_grad, 'grp', split_axis=1, concat_axis=1, tiled=True)]
    all_gather x1 -> x0, blocking collectives: 10.3 us -> none  [shards(): whole_prompts = lax.all_gather(kv_block, 'grp', axis=1, tiled=True)]
    convert_element_type x1 -> x0, local copies, waits for them, and re-layouts: 4.37 us -> none  [attend_block(): d_queries = jnp.einsum('shij,sjhd->sihd', d_scores, key_rows, preferred_e...]
    dot_general x1 -> x0, local copies, waits for them, and re-layouts: 4.36 us -> none  [shards(): jnp.einsum('gsp,sglk->plk', match, arrived, precision=lax.Precision.HIGHEST)]
  transfers between devices with their start and end apart: 4 -> 0, of which waited for: 4 -> 0; matrix products, arithmetic and copies ran while one was open for 9% -> 0% of each run, Pallas kernels for 0% -> 0%
where the time goes in v2:
time: 86.1 us; the launch traced here: 86 us
  Pallas kernels  79.4 us (92%)
  local copies, waits for them, and re-layouts  5.96 us (7%)
    pallas_call x1, Pallas kernels, shards(): pl.pallas_call(kernel, out_shape=(jax.ShapeDtypeStruct((rows, INNER), BF1...  79.4 us
    unnamed x7, local copies, waits for them, and re-layouts  5.96 us

profile of v2, /device:TPU:1, one launch (start us, length us, event | category | flops | bytes accessed | tf_op | source)
XLA Modules:
  0.0 86.0 jit_solution(8252595931906097566)
XLA Ops:
  0.6 79.4 %shard_map.94 = (bf16[1024,1024]{1,0:T(8,128)(2,1)}, bf16[1024,2048]{1,0:T(8,128)(2,1)}, f32[16,4096]{1,0:T(8,128)}) custom-call(s32[512]{0:T(512)} %prompt_ref.1, s32[32]{0:T(128)} %len_ref.1, bf16[16,4096]{1,0:T(8,128)(2,1)} %bitcast.11, bf16[1024,2048]{1,0:T(8,128)(2,1)} %w_hbm.1, bf16[1024,2048]{1,0:T(8,128)(2,1)} %bitcast.6, bf16[2048,1024]{1,0:T(8,128)(2,1)} %qw_hbm.1, ...), custom_call_target="tpu_custom_call" | custom-call | tf_op jit(solution)/shard_map/pallas_call | solution.py:368
  80.0 0.0 copy-start
  80.0 3.2 %copy.13 = bf16[4,256,1024]{2,1,0:T(8,128)(2,1)} copy(bf16[4,256,1024]{2,1,0:T(8,128)(2,1)} %bitcast.9) | data formatting | bytes 4194304
  83.3 0.0 copy-done
  83.3 0.0 copy-start.1
  83.3 2.0 %copy.14 = bf16[4,256,2048]{2,1,0:T(8,128)(2,1)} copy(bf16[4,256,2048]{2,1,0:T(8,128)(2,1)S(1)} %bitcast.7) | data formatting | bytes 8388608
  85.3 0.0 copy-done.1
  85.3 0.7 copy.15
Async XLA Ops:
  80.0 3.2 %copy-start = (bf16[1024,2048]{1,0:T(8,128)(2,1)S(1)}, bf16[1024,2048]{1,0:T(8,128)(2,1)}, u32[]{:S(2)}) copy-start(bf16[1024,2048]{1,0:T(8,128)(2,1)} %get-tuple-element.7) | copy-start | bytes 12582916
  83.3 2.0 %copy-start.1 = (f32[16,4096]{1,0:T(8,128)S(1)}, f32[16,4096]{1,0:T(8,128)}, u32[]{:S(2)}) copy-start(f32[16,4096]{1,0:T(8,128)} %get-tuple-element.8) | copy-start | bytes 786436

commit v3 on v2

v3 whole, which is shorter than its diff:
```python
import math

import jax
import jax.numpy as jnp
from jax import lax
from jax.experimental import pallas as pl
from jax.experimental.pallas import tpu as pltpu
from jax.sharding import PartitionSpec as P

HEADS = 8
HD = 128
NEG_FILL = -1e30
MESH = pl.DeviceIdType.MESH
BF16 = jnp.bfloat16
F32 = jnp.float32
VMEM_LIMIT = 56 * 1024 * 1024

NY, NX, NZ, NC = 4, 4, 4, 2
SAMP = 4
TOK = 16
INNER = 1024
WIDE = 4096
DEPTH = 1024
IMG = 256
CIMG = 2048
PROMPTS = 32
CHUNKS = 4
CW = INNER // CHUNKS
LINE = [(k, j) for k in (2, 1, 3, 0) for j in (1, 0)]
NT = (((1,), (1,)), ((), ()))
TN = (((0,), (0,)), ((), ()))


def place():
    grp = lax.axis_index("grp")
    dev = lax.axis_index("dev")
    return grp, lax.div(dev, 8), lax.rem(lax.div(dev, 2), 4), lax.rem(dev, 2)


def at(grp, x, z, core):
    return {"grp": grp, "dev": (x * NZ + z) * NC + core}


def turn(index, step, size):
    return lax.rem(index + step, size)


def greet():
    y, x, z, c = place()
    barrier = pltpu.get_barrier_semaphore()
    peers = [at(turn(y, k, NY), x, z, turn(c, j, NC)) for k in range(1, NY) for j in range(NC)]
    peers += [
        at(y, turn(x, i, NX), turn(z, j, NZ), turn(c, k, NC))
        for i in range(NX) for j in range(NZ) for k in range(NC) if i or j or k
    ]
    for peer in peers:
        pl.semaphore_signal(barrier, inc=1, device_id=peer, device_id_type=MESH)
    pl.semaphore_wait(barrier, len(peers))


def send(src, dst, send_sem, recv_sem, peer):
    pltpu.make_async_remote_copy(
        src_ref=src, dst_ref=dst, send_sem=send_sem, recv_sem=recv_sem, device_id=peer, device_id_type=MESH
    ).start()


def take(sem, like):
    pltpu.make_async_copy(like, like, sem).wait()


def kernel(
    prompt_ref, len_ref, cap_hbm, w_hbm, x_hbm, qw_hbm, g_hbm, context_out, image_out, caption_out, *scratch
):
    (
        w_v, x_v, qw_v, q_v, g_v, ctx_v, dq_v, caps, part, rs, kvb, sel, skv, dkv, arr, match,
        sums, rsb, r1, kvg, full, cg,
        load_sem, sent, cap_r, rs_r, ag_r, sel_r, grad_r, r1_r, f_r, o_r, store_sem,
    ) = scratch[:-CHUNKS]
    gath = scratch[-CHUNKS:]
    y, x, z, c = place()
    stores = []

    def columns(index):
        return pl.ds(pl.multiple_of(index * DEPTH, DEPTH), DEPTH)

    def keep(src, dst, sem):
        copy = pltpu.make_async_copy(src, dst, sem)
        copy.start()
        return copy

    own_cap = keep(cap_hbm.at[:, columns(y)], caps.at[y], load_sem.at[0])
    load_w = keep(w_hbm, w_v, load_sem.at[1])
    load_qw = keep(qw_hbm, qw_v, load_sem.at[3])
    load_x = keep(x_hbm, x_v, load_sem.at[2])
    greet()

    for k in (2, 1, 3):
        to = turn(y, k, NY)
        send(cap_hbm.at[:, columns(to)], caps.at[y], sent.at[0], cap_r, at(to, x, z, c))
    own_cap.wait()
    load_w.wait()
    take(cap_r, caps.at[pl.ds(0, NY - 1)])
    load_g = keep(g_hbm, g_v, load_sem.at[4])

    def project(tile):
        rows = pl.ds(tile * IMG, IMG)
        q_v[rows, :] = jnp.dot(x_v[rows, :], qw_v[...], preferred_element_type=F32).astype(BF16)

    def partial(q):
        lhs = caps[...].reshape(NY * TOK, DEPTH)
        for half in range(2):
            part[q, :, :, pl.ds(half * CW, CW)] = jnp.dot(
                lhs, w_v[:, pl.ds(half * INNER + q * CW, CW)], preferred_element_type=F32
            ).reshape(NY, TOK, CW)
        for k in (2, 1, 3):
            to = turn(y, k, NY)
            send(part.at[q, to], rs.at[q, k - 1], sent.at[1], rs_r.at[q], at(to, x, z, c))

    me = (x * NZ + z) * NC + c

    def gather(q):
        take(rs_r.at[q], rs.at[q])
        whole = (part[q, y] + rs[q, 0] + rs[q, 1] + rs[q, 2]).astype(BF16)
        kvb[q, 0] = whole[:, :CW]
        kvb[q, 1] = whole[:, CW:]
        for i in (2, 1, 3, 0):
            for j in (2, 1, 3, 0):
                for k in range(NC):
                    if i or j or k:
                        to_c = turn(c, k, NC)
                        send(
                            kvb.at[q, to_c], gath[q].at[me], sent.at[2], ag_r.at[q],
                            at(y, turn(x, i, NX), turn(z, j, NZ), to_c),
                        )
        gath[q][me] = kvb[q, c]

    def select(q):
        take(ag_r.at[q], gath[q].at[pl.ds(0, PROMPTS - 1)])
        for slot, (k, j) in enumerate(LINE):
            to_y, to_c = turn(y, k, NY), turn(c, j, NC)
            start = (to_y * (NX * NZ * NC) + (x * NZ + z) * NC + to_c) * SAMP
            for i in range(SAMP):
                block = gath[q][prompt_ref[start + i]]
                if k or j:
                    sel[q, slot * SAMP + i] = block
                else:
                    skv[q, c, i, y] = block
            if k or j:
                send(sel.at[q, pl.ds(slot * SAMP, SAMP)], skv.at[q, c, :, y], sent.at[3], sel_r.at[q], at(to_y, x, z, to_c))

    count = NY * NC * SAMP * TOK

    def one_hot():
        lanes = lax.broadcasted_iota(jnp.int32, (1, count), 1)
        owner = jnp.zeros((1, count), jnp.int32)
        for yy in range(NY):
            for cc in range(NC):
                for i in range(SAMP):
                    spot = (yy * NC + cc) * SAMP + i
                    p = prompt_ref[(yy * (NX * NZ * NC) + (x * NZ + z) * NC + cc) * SAMP + i]
                    owner = jnp.where(lanes // TOK == spot, p, owner)
        wanted = owner * TOK + lanes % TOK
        ids = lax.broadcasted_iota(jnp.int32, (PROMPTS * TOK, count), 0)
        match[...] = jnp.where(ids == wanted, 1.0, 0.0).astype(BF16)

    partial(0)
    partial(1)
    partial(2)
    partial(3)
    load_qw.wait()
    load_x.wait()
    project(0)
    gather(0)
    gather(1)
    gather(2)
    project(1)
    gather(3)
    project(2)
    select(0)
    project(3)
    select(1)
    select(2)
    select(3)
    one_hot()
    load_g.wait()

    scale = 1.0 / math.sqrt(HD)
    base = (y * (NX * NZ * NC) + (x * NZ + z) * NC + c) * SAMP
    tokens = NY * TOK

    def attention(q, s):
        rows = pl.ds(pl.multiple_of(s * IMG, IMG), IMG)
        cols = pl.ds(q * CW, CW)
        length = len_ref[prompt_ref[base + s]]
        live = lax.broadcasted_iota(jnp.int32, (2, tokens, IMG), 1) < length
        lead = lax.broadcasted_iota(jnp.int32, (tokens, CW), 1) < HD
        queries = q_v[rows, cols]
        grads = g_v[rows, cols]
        key = skv[q, 0, s].reshape(tokens, CW)
        value = skv[q, 1, s].reshape(tokens, CW)
        zero = jnp.zeros_like(key)
        key2 = jnp.concatenate([jnp.where(lead, key, zero), jnp.where(lead, zero, key)], axis=0)
        value2 = jnp.concatenate([jnp.where(lead, value, zero), jnp.where(lead, zero, value)], axis=0)
        scores = lax.dot_general(key2, queries, NT, preferred_element_type=F32) * scale
        scores = jnp.where(live, scores.reshape(2, tokens, IMG), NEG_FILL)
        expd = jnp.exp(scores - jnp.max(scores, axis=1, keepdims=True))
        soft = expd * (1.0 / jnp.sum(expd, axis=1, keepdims=True))
        soft_b = soft.astype(BF16).reshape(2 * tokens, IMG)
        d_soft = lax.dot_general(value2, grads, NT, preferred_element_type=F32).reshape(2, tokens, IMG)
        inner = jnp.sum(d_soft * soft, axis=1, keepdims=True)
        d_scores = (soft * (d_soft - inner) * scale).astype(BF16).reshape(2 * tokens, IMG)
        ctx_v[rows, cols] = lax.dot_general(soft_b, value2, TN, preferred_element_type=F32).astype(BF16)
        dq_v[rows, cols] = lax.dot_general(d_scores, key2, TN, preferred_element_type=F32).astype(BF16)
        d_key = jnp.dot(d_scores, queries, preferred_element_type=F32)
        d_value = jnp.dot(soft_b, grads, preferred_element_type=F32)
        dkv[q, 0, s] = jnp.where(lead, d_key[:tokens], d_key[tokens:]).astype(BF16).reshape(NY, TOK, CW)
        dkv[q, 1, s] = jnp.where(lead, d_value[:tokens], d_value[tokens:]).astype(BF16).reshape(NY, TOK, CW)

    seven = pl.ds(0, (NY * NC - 1) * SAMP)

    def attend(q):
        take(sel_r.at[q], sel.at[q, seven])

        def two(t, carry):
            attention(q, 2 * t)
            attention(q, 2 * t + 1)
            return carry

        lax.fori_loop(0, SAMP // 2, two, 0)
        for k, j in LINE[:-1]:
            to_y, to_c = turn(y, k, NY), turn(c, j, NC)
            send(dkv.at[q, to_c, :, to_y], arr.at[q, y, c], sent.at[4], grad_r.at[q], at(to_y, x, z, to_c))
        arr[q, y, c] = dkv[q, c, :, y]
        cols = pl.ds(q * CW, CW)
        stores.append(keep(ctx_v.at[:, cols], context_out.at[:, cols], store_sem.at[q]))

    def add_up(q):
        take(grad_r.at[q], sel.at[q, seven])
        total = jnp.dot(match[...], arr[q].reshape(count, CW), preferred_element_type=F32)
        total = total.reshape(NX, NZ, NC, TOK, CW)
        sums[q] = total
        rsb[q] = total.astype(BF16)
        for i in (2, 1, 3, 0):
            for j in (2, 1, 3, 0):
                if i or j:
                    to_x, to_z = turn(x, i, NX), turn(z, j, NZ)
                    send(
                        rsb.at[q, to_x, to_z], r1.at[q, i * NZ + j - 1], sent.at[5], r1_r.at[q],
                        at(y, to_x, to_z, c),
                    )

    def spread(q):
        take(r1_r.at[q], r1.at[q])
        own = sums[q, x, z]
        for slot in range(NX * NZ - 1):
            own = own + r1[q, slot].astype(F32)
        kvg[q] = own.astype(BF16)
        for k, j in LINE[:-1]:
            to_y, to_c = turn(y, k, NY), turn(c, j, NC)
            send(kvg.at[q, to_c], full.at[q, c, y], sent.at[6], f_r.at[q], at(to_y, x, z, to_c))
        full[q, c, y] = kvg[q, c]

    def finish(q):
        take(f_r.at[q], gath[q].at[pl.ds(0, NY * NC - 1)])
        term = None
        for half in range(2):
            more = lax.dot_general(
                full[q, half].reshape(tokens, CW), w_v[:, pl.ds(half * INNER + q * CW, CW)], NT,
                preferred_element_type=F32,
            )
            term = more if term is None else term + more
        term = term.reshape(NY, TOK, DEPTH)
        cg[...] = term if q == 0 else cg[...] + term

    def image(tile):
        rows = pl.ds(tile * IMG, IMG)
        x_v[rows, :] = lax.dot_general(dq_v[rows, :], qw_v[...], NT, preferred_element_type=F32).astype(BF16)
        stores.append(keep(x_v.at[rows], image_out.at[rows], store_sem.at[CHUNKS + tile]))

    attend(0)
    attend(1)
    attend(2)
    attend(3)
    add_up(0)
    image(0)
    add_up(1)
    add_up(2)
    image(1)
    spread(0)
    add_up(3)
    spread(1)
    image(2)
    finish(0)
    spread(2)
    finish(1)
    spread(3)
    finish(2)
    image(3)
    finish(3)
    for k in (2, 1, 3):
        to = turn(y, k, NY)
        send(cg.at[to], caption_out.at[:, columns(y)], sent.at[7], o_r, at(to, x, z, c))
    stores.append(keep(cg.at[y], caption_out.at[:, columns(y)], store_sem.at[CHUNKS + SAMP]))
    take(sent.at[0], caps.at[pl.ds(0, NY - 1)])
    take(sent.at[1], rs)
    take(sent.at[2], sel.at[:, pl.ds(0, PROMPTS - 1)])
    take(sent.at[3], sel.at[:, seven])
    take(sent.at[4], sel.at[:, seven])
    take(sent.at[5], r1)
    take(sent.at[6], sel.at[0, seven])
    for store in stores:
        store.wait()
    take(o_r, cg.at[pl.ds(0, NY - 1)])
    take(sent.at[7], cg.at[pl.ds(0, NY - 1)])


def shards(captions, kv_weight, image_tokens, q_weight, context_grad, sample_prompt, caption_len):
    any_space = pl.BlockSpec(memory_space=pl.ANY)
    smem = pl.BlockSpec(memory_space=pltpu.SMEM)
    dma = pltpu.SemaphoreType.DMA
    rows = SAMP * IMG

    context, image_grad, caption_grad = pl.pallas_call(
        kernel,
        out_shape=(
            jax.ShapeDtypeStruct((rows, INNER), BF16),
            jax.ShapeDtypeStruct((rows, CIMG), BF16),
            jax.ShapeDtypeStruct((TOK, WIDE), F32),
        ),
        in_specs=[smem, smem] + [any_space] * 5,
        out_specs=(any_space,) * 3,
        scratch_shapes=[
            pltpu.VMEM((DEPTH, 2 * INNER), BF16),
            pltpu.VMEM((rows, CIMG), BF16),
            pltpu.VMEM((CIMG, INNER), BF16),
            pltpu.VMEM((rows, INNER), BF16),
            pltpu.VMEM((rows, INNER), BF16),
            pltpu.VMEM((rows, INNER), BF16),
            pltpu.VMEM((rows, INNER), BF16),
            pltpu.VMEM((NY, TOK, DEPTH), BF16),
            pltpu.VMEM((CHUNKS, NY, TOK, 2 * CW), F32),
            pltpu.VMEM((CHUNKS, NY - 1, TOK, 2 * CW), F32),
            pltpu.VMEM((CHUNKS, 2, TOK, CW), BF16),
            pltpu.VMEM((CHUNKS, NY * NC * SAMP, TOK, CW), BF16),
            pltpu.VMEM((CHUNKS, 2, SAMP, NY, TOK, CW), BF16),
            pltpu.VMEM((CHUNKS, 2, SAMP, NY, TOK, CW), BF16),
            pltpu.VMEM((CHUNKS, NY, NC, SAMP, TOK, CW), BF16),
            pltpu.VMEM((PROMPTS * TOK, NY * NC * SAMP * TOK), BF16),
            pltpu.VMEM((CHUNKS, NX, NZ, NC, TOK, CW), F32),
            pltpu.VMEM((CHUNKS, NX, NZ, NC, TOK, CW), BF16),
            pltpu.VMEM((CHUNKS, NX * NZ - 1, NC, TOK, CW), BF16),
            pltpu.VMEM((CHUNKS, NC, TOK, CW), BF16),
            pltpu.VMEM((CHUNKS, 2, NY, TOK, CW), BF16),
            pltpu.VMEM((NY, TOK, DEPTH), F32),
            dma((5,)),
            dma((8,)),
            dma,
            dma((CHUNKS,)),
            dma((CHUNKS,)),
            dma((CHUNKS,)),
            dma((CHUNKS,)),
            dma((CHUNKS,)),
            dma((CHUNKS,)),
            dma,
            dma((CHUNKS + SAMP + 1,)),
        ] + [pltpu.VMEM((PROMPTS, TOK, CW), BF16) for _ in range(CHUNKS)],
        compiler_params=pltpu.CompilerParams(
            collective_id=0, has_side_effects=True, vmem_limit_bytes=VMEM_LIMIT
        ),
    )(
        sample_prompt,
        caption_len,
        captions.reshape(TOK, WIDE),
        kv_weight,
        image_tokens.reshape(rows, CIMG),
        q_weight,
        context_grad.reshape(rows, INNER),
    )
    return (
        context.reshape(SAMP, IMG, INNER),
        image_grad.reshape(SAMP, IMG, CIMG),
        caption_grad.reshape(1, TOK, WIDE),
    )


def solution(mesh):
    placed = (
        P("dev", "grp", None),
        P("grp", None),
        P(("grp", "dev"), None, None),
        P(),
        P(("grp", "dev"), None, None),
        P(),
        P(),
    )
    return jax.shard_map(
        shards,
        mesh=mesh,
        in_specs=placed,
        out_specs=(
            P(("grp", "dev"), None, None),
            P(("grp", "dev"), None, None),
            P("dev", "grp", None),
        ),
        check_vma=False,
    )
```

time: 86.1 us -> 72.7 us (0.84)
  Pallas kernels: 79.4 us -> 66 us
    pallas_call x1, Pallas kernels: 79.4 us -> 66 us  [shards(): pl.pallas_call(kernel, out_shape=(jax.ShapeDtypeStruct((rows, INNER), BF1...]
where the time goes in v3:
time: 72.7 us; the launch traced here: 72.6 us
  Pallas kernels  66 us (91%)
  local copies, waits for them, and re-layouts  5.96 us (8%)
    pallas_call x1, Pallas kernels, shards(): pl.pallas_call(kernel, out_shape=(jax.ShapeDtypeStruct((rows, INNER), BF1...  66 us
    unnamed x7, local copies, waits for them, and re-layouts  5.96 us

profile of v3, /device:TPU:1, one launch (start us, length us, event | category | flops | bytes accessed | tf_op | source)
XLA Modules:
  0.0 72.6 jit_solution(16864121123771783174)
XLA Ops:
  0.6 66.0 %shard_map.94 = (bf16[1024,1024]{1,0:T(8,128)(2,1)}, bf16[1024,2048]{1,0:T(8,128)(2,1)}, f32[16,4096]{1,0:T(8,128)}) custom-call(s32[512]{0:T(512)} %prompt_ref.1, s32[32]{0:T(128)} %len_ref.1, bf16[16,4096]{1,0:T(8,128)(2,1)} %bitcast.11, bf16[1024,2048]{1,0:T(8,128)(2,1)} %w_hbm.1, bf16[1024,2048]{1,0:T(8,128)(2,1)} %bitcast.6, bf16[2048,1024]{1,0:T(8,128)(2,1)} %qw_hbm.1, ...), custom_call_target="tpu_custom_call" | custom-call | tf_op jit(solution)/shard_map/pallas_call | solution.py:323
  66.6 0.0 copy-start
  66.6 3.2 %copy.13 = bf16[4,256,1024]{2,1,0:T(8,128)(2,1)} copy(bf16[4,256,1024]{2,1,0:T(8,128)(2,1)} %bitcast.9) | data formatting | bytes 4194304
  69.8 0.0 copy-done
  69.8 0.0 copy-start.1
  69.8 2.0 %copy.14 = bf16[4,256,2048]{2,1,0:T(8,128)(2,1)} copy(bf16[4,256,2048]{2,1,0:T(8,128)(2,1)S(1)} %bitcast.7) | data formatting | bytes 8388608
  71.9 0.0 copy-done.1
  71.9 0.7 copy.15
Async XLA Ops:
  66.6 3.2 %copy-start = (bf16[1024,2048]{1,0:T(8,128)(2,1)S(1)}, bf16[1024,2048]{1,0:T(8,128)(2,1)}, u32[]{:S(2)}) copy-start(bf16[1024,2048]{1,0:T(8,128)(2,1)} %get-tuple-element.7) | copy-start | bytes 12582916
  69.8 2.0 %copy-start.1 = (f32[16,4096]{1,0:T(8,128)S(1)}, f32[16,4096]{1,0:T(8,128)}, u32[]{:S(2)}) copy-start(f32[16,4096]{1,0:T(8,128)} %get-tuple-element.8) | copy-start | bytes 786436

commit v4 on v3

--- a/solution.py
+++ b/solution.py
@@ -13,7 +13,7 @@
 MESH = pl.DeviceIdType.MESH
 BF16 = jnp.bfloat16
 F32 = jnp.float32
-VMEM_LIMIT = 56 * 1024 * 1024
+VMEM_LIMIT = 44 * 1024 * 1024
 
 NY, NX, NZ, NC = 4, 4, 4, 2
 SAMP = 4
@@ -48,14 +48,26 @@
 def greet():
     y, x, z, c = place()
     barrier = pltpu.get_barrier_semaphore()
-    peers = [at(turn(y, k, NY), x, z, turn(c, j, NC)) for k in range(1, NY) for j in range(NC)]
-    peers += [
-        at(y, turn(x, i, NX), turn(z, j, NZ), turn(c, k, NC))
-        for i in range(NX) for j in range(NZ) for k in range(NC) if i or j or k
-    ]
+    peers = [at(turn(y, k, NY), x, z, c) for k in range(1, NY)]
+    peers += [at(y, turn(x, k, NX), z, c) for k in range(1, NX)]
+    peers += [at(y, x, turn(z, k, NZ), c) for k in range(1, NZ)]
+    peers += [at(y, x, z, 1 - c)]
     for peer in peers:
         pl.semaphore_signal(barrier, inc=1, device_id=peer, device_id_type=MESH)
     pl.semaphore_wait(barrier, len(peers))
+
+
+def pass_on(line_sem):
+    y, x, z, c = place()
+    for k in range(1, NX):
+        pl.semaphore_signal(line_sem, inc=1, device_id=at(y, turn(x, k, NX), z, c), device_id_type=MESH)
+
+
+def hear(line_sem, pair_sem):
+    y, x, z, c = place()
+    pl.semaphore_wait(line_sem, NX - 1)
+    pl.semaphore_signal(pair_sem, inc=1, device_id=at(y, x, z, 1 - c), device_id_type=MESH)
+    pl.semaphore_wait(pair_sem, 1)
 
 
 def send(src, dst, send_sem, recv_sem, peer):
@@ -69,16 +81,15 @@
 
 
 def kernel(
-    prompt_ref, len_ref, cap_hbm, w_hbm, x_hbm, qw_hbm, g_hbm, context_out, image_out, caption_out, *scratch
+    prompt_hbm, len_hbm, cap_hbm, w_hbm, x_hbm, qw_hbm, g_hbm, context_out, image_out, caption_out, *scratch
 ):
     (
-        w_v, x_v, qw_v, q_v, g_v, ctx_v, dq_v, caps, part, rs, kvb, sel, skv, dkv, arr, match,
+        prompt_ref, len_ref, w_v, x_v, qw_v, q_v, g_v, dq_v, cap_v, caps, part, rs, kvb, sel, skv, dkv, arr, match,
         sums, rsb, r1, kvg, full, cg,
-        load_sem, sent, cap_r, rs_r, ag_r, sel_r, grad_r, r1_r, f_r, o_r, store_sem,
+        load_sem, sent, cap_r, rs_r, ag_r, sel_r, grad_r, r1_r, f_r, o_r, line_sem, pair_sem,
     ) = scratch[:-CHUNKS]
     gath = scratch[-CHUNKS:]
     y, x, z, c = place()
-    stores = []
 
     def columns(index):
         return pl.ds(pl.multiple_of(index * DEPTH, DEPTH), DEPTH)
@@ -88,19 +99,23 @@
         copy.start()
         return copy
 
-    own_cap = keep(cap_hbm.at[:, columns(y)], caps.at[y], load_sem.at[0])
+    load_cap = keep(cap_hbm, cap_v, load_sem.at[0])
+    load_prompt = keep(prompt_hbm, prompt_ref, load_sem.at[5])
+    load_len = keep(len_hbm, len_ref, load_sem.at[6])
     load_w = keep(w_hbm, w_v, load_sem.at[1])
+    load_cap.wait()
+    greet()
+
+    for k in (2, 1, 3):
+        to = turn(y, k, NY)
+        send(cap_v.at[:, columns(to)], caps.at[y], sent.at[0], cap_r, at(to, x, z, c))
+    caps[y] = cap_v[:, columns(y)]
+    pass_on(line_sem)
+    load_w.wait()
     load_qw = keep(qw_hbm, qw_v, load_sem.at[3])
     load_x = keep(x_hbm, x_v, load_sem.at[2])
-    greet()
-
-    for k in (2, 1, 3):
-        to = turn(y, k, NY)
-        send(cap_hbm.at[:, columns(to)], caps.at[y], sent.at[0], cap_r, at(to, x, z, c))
-    own_cap.wait()
-    load_w.wait()
     take(cap_r, caps.at[pl.ds(0, NY - 1)])
-    load_g = keep(g_hbm, g_v, load_sem.at[4])
+    hear(line_sem, pair_sem)
 
     def project(tile):
         rows = pl.ds(tile * IMG, IMG)
@@ -164,20 +179,23 @@
         match[...] = jnp.where(ids == wanted, 1.0, 0.0).astype(BF16)
 
     partial(0)
+    load_prompt.wait()
+    load_len.wait()
+    load_qw.wait()
+    load_x.wait()
+    load_g = keep(g_hbm, g_v, load_sem.at[4])
+    project(0)
     partial(1)
+    project(1)
+    gather(0)
     partial(2)
     partial(3)
-    load_qw.wait()
-    load_x.wait()
-    project(0)
-    gather(0)
     gather(1)
+    project(2)
     gather(2)
-    project(1)
-    gather(3)
-    project(2)
     select(0)
     project(3)
+    gather(3)
     select(1)
     select(2)
     select(3)
@@ -209,7 +227,7 @@
         d_soft = lax.dot_general(value2, grads, NT, preferred_element_type=F32).reshape(2, tokens, IMG)
         inner = jnp.sum(d_soft * soft, axis=1, keepdims=True)
         d_scores = (soft * (d_soft - inner) * scale).astype(BF16).reshape(2 * tokens, IMG)
-        ctx_v[rows, cols] = lax.dot_general(soft_b, value2, TN, preferred_element_type=F32).astype(BF16)
+        context_out[rows, cols] = lax.dot_general(soft_b, value2, TN, preferred_element_type=F32).astype(BF16)
         dq_v[rows, cols] = lax.dot_general(d_scores, key2, TN, preferred_element_type=F32).astype(BF16)
         d_key = jnp.dot(d_scores, queries, preferred_element_type=F32)
         d_value = jnp.dot(soft_b, grads, preferred_element_type=F32)
@@ -231,8 +249,6 @@
             to_y, to_c = turn(y, k, NY), turn(c, j, NC)
             send(dkv.at[q, to_c, :, to_y], arr.at[q, y, c], sent.at[4], grad_r.at[q], at(to_y, x, z, to_c))
         arr[q, y, c] = dkv[q, c, :, y]
-        cols = pl.ds(q * CW, CW)
-        stores.append(keep(ctx_v.at[:, cols], context_out.at[:, cols], store_sem.at[q]))
 
     def add_up(q):
         take(grad_r.at[q], sel.at[q, seven])
@@ -274,8 +290,7 @@
 
     def image(tile):
         rows = pl.ds(tile * IMG, IMG)
-        x_v[rows, :] = lax.dot_general(dq_v[rows, :], qw_v[...], NT, preferred_element_type=F32).astype(BF16)
-        stores.append(keep(x_v.at[rows], image_out.at[rows], store_sem.at[CHUNKS + tile]))
+        image_out[rows, :] = lax.dot_general(dq_v[rows, :], qw_v[...], NT, preferred_element_type=F32).astype(BF16)
 
     attend(0)
     attend(1)
@@ -300,7 +315,7 @@
     for k in (2, 1, 3):
         to = turn(y, k, NY)
         send(cg.at[to], caption_out.at[:, columns(y)], sent.at[7], o_r, at(to, x, z, c))
-    stores.append(keep(cg.at[y], caption_out.at[:, columns(y)], store_sem.at[CHUNKS + SAMP]))
+    caption_out[:, columns(y)] = cg[y]
     take(sent.at[0], caps.at[pl.ds(0, NY - 1)])
     take(sent.at[1], rs)
     take(sent.at[2], sel.at[:, pl.ds(0, PROMPTS - 1)])
@@ -308,35 +323,35 @@
     take(sent.at[4], sel.at[:, seven])
     take(sent.at[5], r1)
     take(sent.at[6], sel.at[0, seven])
-    for store in stores:
-        store.wait()
     take(o_r, cg.at[pl.ds(0, NY - 1)])
     take(sent.at[7], cg.at[pl.ds(0, NY - 1)])
 
 
 def shards(captions, kv_weight, image_tokens, q_weight, context_grad, sample_prompt, caption_len):
-    any_space = pl.BlockSpec(memory_space=pl.ANY)
-    smem = pl.BlockSpec(memory_space=pltpu.SMEM)
+    hbm = pl.BlockSpec(memory_space=pltpu.HBM)
+    vmem = pl.BlockSpec(memory_space=pltpu.VMEM)
     dma = pltpu.SemaphoreType.DMA
     rows = SAMP * IMG
 
     context, image_grad, caption_grad = pl.pallas_call(
         kernel,
         out_shape=(
-            jax.ShapeDtypeStruct((rows, INNER), BF16),
-            jax.ShapeDtypeStruct((rows, CIMG), BF16),
-            jax.ShapeDtypeStruct((TOK, WIDE), F32),
+            pltpu.VMEM((rows, INNER), BF16),
+            pltpu.VMEM((rows, CIMG), BF16),
+            pltpu.VMEM((TOK, WIDE), F32),
         ),
-        in_specs=[smem, smem] + [any_space] * 5,
-        out_specs=(any_space,) * 3,
+        in_specs=[hbm] * 7,
+        out_specs=(vmem,) * 3,
         scratch_shapes=[
+            pltpu.SMEM(sample_prompt.shape, jnp.int32),
+            pltpu.SMEM(caption_len.shape, jnp.int32),
             pltpu.VMEM((DEPTH, 2 * INNER), BF16),
             pltpu.VMEM((rows, CIMG), BF16),
             pltpu.VMEM((CIMG, INNER), BF16),
             pltpu.VMEM((rows, INNER), BF16),
             pltpu.VMEM((rows, INNER), BF16),
             pltpu.VMEM((rows, INNER), BF16),
-            pltpu.VMEM((rows, INNER), BF16),
+            pltpu.VMEM((TOK, WIDE), BF16),
             pltpu.VMEM((NY, TOK, DEPTH), BF16),
             pltpu.VMEM((CHUNKS, NY, TOK, 2 * CW), F32),
             pltpu.VMEM((CHUNKS, NY - 1, TOK, 2 * CW), F32),
@@ -352,7 +367,7 @@
             pltpu.VMEM((CHUNKS, NC, TOK, CW), BF16),
             pltpu.VMEM((CHUNKS, 2, NY, TOK, CW), BF16),
             pltpu.VMEM((NY, TOK, DEPTH), F32),
-            dma((5,)),
+            dma((7,)),
             dma((8,)),
             dma,
             dma((CHUNKS,)),
@@ -362,20 +377,24 @@
             dma((CHUNKS,)),
             dma((CHUNKS,)),
             dma,
-            dma((CHUNKS + SAMP + 1,)),
+            pltpu.SemaphoreType.REGULAR,
+            pltpu.SemaphoreType.REGULAR,
         ] + [pltpu.VMEM((PROMPTS, TOK, CW), BF16) for _ in range(CHUNKS)],
         compiler_params=pltpu.CompilerParams(
             collective_id=0, has_side_effects=True, vmem_limit_bytes=VMEM_LIMIT
         ),
-    )(
-        sample_prompt,
-        caption_len,
-        captions.reshape(TOK, WIDE),
-        kv_weight,
-        image_tokens.reshape(rows, CIMG),
-        q_weight,
-        context_grad.reshape(rows, INNER),
-    )
+    )(*[
+        pltpu.with_memory_space_constraint(operand, pltpu.HBM)
+        for operand in (
+            sample_prompt,
+            caption_len,
+            captions.reshape(TOK, WIDE),
+            kv_weight,
+            image_tokens.reshape(rows, CIMG),
+            q_weight,
+            context_grad.reshape(rows, INNER),
+        )
+    ])
     return (
         context.reshape(SAMP, IMG, INNER),
         image_grad.reshape(SAMP, IMG, CIMG),

time: 72.7 us -> 69.1 us (0.950)
  local copies, waits for them, and re-layouts: 5.96 us -> 4.04 us
  Pallas kernels: 66 us -> 64.3 us
    unnamed x7 -> x3, local copies, waits for them, and re-layouts: 5.96 us -> 4.04 us
    pallas_call x1, Pallas kernels: 66 us -> 64.3 us  [shards(): pl.pallas_call(kernel, out_shape=(pltpu.VMEM((rows, INNER), BF16), pltpu....]
where the time goes in v4:
time: 69.1 us; the launch traced here: 69 us
  Pallas kernels  64.3 us (93%)
  local copies, waits for them, and re-layouts  4.04 us (6%)
    pallas_call x1, Pallas kernels, shards(): pl.pallas_call(kernel, out_shape=(pltpu.VMEM((rows, INNER), BF16), pltpu....  64.3 us
    unnamed x3, local copies, waits for them, and re-layouts  4.04 us

profile of v4, /device:TPU:1, one launch (start us, length us, event | category | flops | bytes accessed | tf_op | source)
XLA Modules:
  0.0 69.0 jit_solution(11411212868099323283)
XLA Ops:
  0.6 64.3 %shard_map.94 = (bf16[1024,1024]{1,0:T(8,128)(2,1)S(1)}, bf16[1024,2048]{1,0:T(8,128)(2,1)S(1)}, f32[16,4096]{1,0:T(8,128)S(1)}) custom-call(s32[512]{0:T(512)} %prompt_hbm.1, s32[32]{0:T(128)} %len_hbm.1, bf16[16,4096]{1,0:T(8,128)(2,1)} %bitcast.11, bf16[1024,2048]{1,0:T(8,128)(2,1)} %w_hbm.1, bf16[1024,2048]{1,0:T(8,128)(2,1)} %bitcast.9, ...), custom_call_target="tpu_custom_call" | custom-call | tf_op jit(solution)/shard_map/pallas_call | solution.py:336
  65.0 1.3 %copy.13 = bf16[4,256,1024]{2,1,0:T(8,128)(2,1)} copy(bf16[4,256,1024]{2,1,0:T(8,128)(2,1)S(1)} %bitcast.7) | data formatting | bytes 4194304
  66.3 2.0 %copy.14 = bf16[4,256,2048]{2,1,0:T(8,128)(2,1)} copy(bf16[4,256,2048]{2,1,0:T(8,128)(2,1)S(1)} %bitcast.6) | data formatting | bytes 8388608
  68.3 0.7 %copy.15 = f32[1,16,4096]{2,1,0:T(8,128)} copy(f32[1,16,4096]{2,1,0:T(8,128)S(1)} %bitcast.8) | data formatting | bytes 524288

commit v5 on v4

--- a/solution.py
+++ b/solution.py
@@ -85,8 +85,8 @@
 ):
     (
         prompt_ref, len_ref, w_v, x_v, qw_v, q_v, g_v, dq_v, cap_v, caps, part, rs, kvb, sel, skv, dkv, arr, match,
-        sums, rsb, r1, kvg, full, cg,
-        load_sem, sent, cap_r, rs_r, ag_r, sel_r, grad_r, r1_r, f_r, o_r, line_sem, pair_sem,
+        sums, rsb, r1, kvg, full, cg, late, late_b, early, late_in,
+        load_sem, sent, cap_r, rs_r, ag_r, sel_r, grad_r, r1_r, f_r, o_r, early_r, line_sem, pair_sem,
     ) = scratch[:-CHUNKS]
     gath = scratch[-CHUNKS:]
     y, x, z, c = place()
@@ -286,7 +286,8 @@
             )
             term = more if term is None else term + more
         term = term.reshape(NY, TOK, DEPTH)
-        cg[...] = term if q == 0 else cg[...] + term
+        held = cg if q < CHUNKS // 2 else late
+        held[...] = term if q % (CHUNKS // 2) == 0 else held[...] + term
 
     def image(tile):
         rows = pl.ds(tile * IMG, IMG)
@@ -308,14 +309,18 @@
     finish(0)
     spread(2)
     finish(1)
+    for k in (2, 1, 3):
+        to = turn(y, k, NY)
+        send(cg.at[to], early.at[k - 1], sent.at[7], early_r, at(to, x, z, c))
     spread(3)
     finish(2)
     image(3)
     finish(3)
+    late_b[...] = late[...].astype(BF16)
     for k in (2, 1, 3):
         to = turn(y, k, NY)
-        send(cg.at[to], caption_out.at[:, columns(y)], sent.at[7], o_r, at(to, x, z, c))
-    caption_out[:, columns(y)] = cg[y]
+        send(late_b.at[to], late_in.at[k - 1], sent.at[8], o_r, at(to, x, z, c))
+    caption_out[:, columns(y)] = cg[y] + late[y]
     take(sent.at[0], caps.at[pl.ds(0, NY - 1)])
     take(sent.at[1], rs)
     take(sent.at[2], sel.at[:, pl.ds(0, PROMPTS - 1)])
@@ -323,8 +328,12 @@
     take(sent.at[4], sel.at[:, seven])
     take(sent.at[5], r1)
     take(sent.at[6], sel.at[0, seven])
-    take(o_r, cg.at[pl.ds(0, NY - 1)])
-    take(sent.at[7], cg.at[pl.ds(0, NY - 1)])
+    take(early_r, early)
+    take(o_r, late_in)
+    for k in range(1, NY):
+        caption_out[:, columns(turn(y, NY - k, NY))] = early[k - 1] + late_in[k - 1].astype(F32)
+    take(sent.at[7], early)
+    take(sent.at[8], late_in)
 
 
 def shards(captions, kv_weight, image_tokens, q_weight, context_grad, sample_prompt, caption_len):
@@ -367,8 +376,12 @@
             pltpu.VMEM((CHUNKS, NC, TOK, CW), BF16),
             pltpu.VMEM((CHUNKS, 2, NY, TOK, CW), BF16),
             pltpu.VMEM((NY, TOK, DEPTH), F32),
+            pltpu.VMEM((NY, TOK, DEPTH), F32),
+            pltpu.VMEM((NY, TOK, DEPTH), BF16),
+            pltpu.VMEM((NY - 1, TOK, DEPTH), F32),
+            pltpu.VMEM((NY - 1, TOK, DEPTH), BF16),
             dma((7,)),
-            dma((8,)),
+            dma((9,)),
             dma,
             dma((CHUNKS,)),
             dma((CHUNKS,)),
@@ -376,6 +389,7 @@
             dma((CHUNKS,)),
             dma((CHUNKS,)),
             dma((CHUNKS,)),
+            dma,
             dma,
             pltpu.SemaphoreType.REGULAR,
             pltpu.SemaphoreType.REGULAR,

time: 69.1 us -> 68.2 us (0.987)
  Pallas kernels: 64.3 us -> 63.4 us
    pallas_call x1, Pallas kernels: 64.3 us -> 63.4 us  [shards(): pl.pallas_call(kernel, out_shape=(pltpu.VMEM((rows, INNER), BF16), pltpu....]
where the time goes in v5:
time: 68.2 us; the launch traced here: 68.1 us
  Pallas kernels  63.4 us (93%)
  local copies, waits for them, and re-layouts  4.04 us (6%)
    pallas_call x1, Pallas kernels, shards(): pl.pallas_call(kernel, out_shape=(pltpu.VMEM((rows, INNER), BF16), pltpu....  63.4 us
    unnamed x3, local copies, waits for them, and re-layouts  4.04 us

profile of v5, /device:TPU:1, one launch (start us, length us, event | category | flops | bytes accessed | tf_op | source)
XLA Modules:
  0.0 68.1 jit_solution(9348171192495445198)
XLA Ops:
  0.6 63.4 %shard_map.94 = (bf16[1024,1024]{1,0:T(8,128)(2,1)S(1)}, bf16[1024,2048]{1,0:T(8,128)(2,1)S(1)}, f32[16,4096]{1,0:T(8,128)S(1)}) custom-call(s32[512]{0:T(512)} %prompt_hbm.1, s32[32]{0:T(128)} %len_hbm.1, bf16[16,4096]{1,0:T(8,128)(2,1)} %bitcast.11, bf16[1024,2048]{1,0:T(8,128)(2,1)} %w_hbm.1, bf16[1024,2048]{1,0:T(8,128)(2,1)} %bitcast.9, ...), custom_call_target="tpu_custom_call" | custom-call | tf_op jit(solution)/shard_map/pallas_call | solution.py:345
  64.1 1.3 %copy.13 = bf16[4,256,1024]{2,1,0:T(8,128)(2,1)} copy(bf16[4,256,1024]{2,1,0:T(8,128)(2,1)S(1)} %bitcast.7) | data formatting | bytes 4194304
  65.4 2.0 %copy.14 = bf16[4,256,2048]{2,1,0:T(8,128)(2,1)} copy(bf16[4,256,2048]{2,1,0:T(8,128)(2,1)S(1)} %bitcast.6) | data formatting | bytes 8388608
  67.4 0.7 %copy.15 = f32[1,16,4096]{2,1,0:T(8,128)} copy(f32[1,16,4096]{2,1,0:T(8,128)S(1)} %bitcast.8) | data formatting | bytes 524288

commit v6 on v5

--- a/solution.py
+++ b/solution.py
@@ -103,8 +103,8 @@
     load_prompt = keep(prompt_hbm, prompt_ref, load_sem.at[5])
     load_len = keep(len_hbm, len_ref, load_sem.at[6])
     load_w = keep(w_hbm, w_v, load_sem.at[1])
+    greet()
     load_cap.wait()
-    greet()
 
     for k in (2, 1, 3):
         to = turn(y, k, NY)
@@ -114,8 +114,8 @@
     load_w.wait()
     load_qw = keep(qw_hbm, qw_v, load_sem.at[3])
     load_x = keep(x_hbm, x_v, load_sem.at[2])
+    hear(line_sem, pair_sem)
     take(cap_r, caps.at[pl.ds(0, NY - 1)])
-    hear(line_sem, pair_sem)
 
     def project(tile):
         rows = pl.ds(tile * IMG, IMG)

time: 68.2 us -> 67.2 us (0.985)
  Pallas kernels: 63.4 us -> 62.2 us
    pallas_call x1, Pallas kernels: 63.4 us -> 62.2 us  [shards(): pl.pallas_call(kernel, out_shape=(pltpu.VMEM((rows, INNER), BF16), pltpu....]
where the time goes in v6:
time: 67.2 us; the launch traced here: 66.9 us
  Pallas kernels  62.2 us (93%)
  local copies, waits for them, and re-layouts  4.04 us (6%)
    pallas_call x1, Pallas kernels, shards(): pl.pallas_call(kernel, out_shape=(pltpu.VMEM((rows, INNER), BF16), pltpu....  62.2 us
    unnamed x3, local copies, waits for them, and re-layouts  4.04 us

profile of v6, /device:TPU:1, one launch (start us, length us, event | category | flops | bytes accessed | tf_op | source)
XLA Modules:
  0.0 66.9 jit_solution(3557841808373633495)
XLA Ops:
  0.6 62.2 %shard_map.94 = (bf16[1024,1024]{1,0:T(8,128)(2,1)S(1)}, bf16[1024,2048]{1,0:T(8,128)(2,1)S(1)}, f32[16,4096]{1,0:T(8,128)S(1)}) custom-call(s32[512]{0:T(512)} %prompt_hbm.1, s32[32]{0:T(128)} %len_hbm.1, bf16[16,4096]{1,0:T(8,128)(2,1)} %bitcast.11, bf16[1024,2048]{1,0:T(8,128)(2,1)} %w_hbm.1, bf16[1024,2048]{1,0:T(8,128)(2,1)} %bitcast.9, ...), custom_call_target="tpu_custom_call" | custom-call | tf_op jit(solution)/shard_map/pallas_call | solution.py:345
  62.9 1.3 %copy.13 = bf16[4,256,1024]{2,1,0:T(8,128)(2,1)} copy(bf16[4,256,1024]{2,1,0:T(8,128)(2,1)S(1)} %bitcast.7) | data formatting | bytes 4194304
  64.2 2.0 %copy.14 = bf16[4,256,2048]{2,1,0:T(8,128)(2,1)} copy(bf16[4,256,2048]{2,1,0:T(8,128)(2,1)S(1)} %bitcast.6) | data formatting | bytes 8388608
  66.2 0.7 %copy.15 = f32[1,16,4096]{2,1,0:T(8,128)} copy(f32[1,16,4096]{2,1,0:T(8,128)S(1)} %bitcast.8) | data formatting | bytes 524288
